TPU v7x, 32 devices: a whole 2x2x4 slice. The times are simulated.
32 devices in a mesh: gx: 8 (over z, x), gy: 4 (over y, core).
Axes of the slice: x: 2, y: 2, z: 4, core: 2. Of those that a mesh axis runs over, the one named last changes fastest.
Arguments:
- velocity: float32 [3, 256, 4, 512], P(None, 'gx', None, 'gy'), may hold values from -6 to 6
- pair_blocks: float32 [8, 4, 256, 128], P('gx', 'gy'), may hold values from 0.1 to 2
- send_up: int32 [8, 4, 128], P('gx', 'gy'), may hold values from 0 to 255
- send_side: int32 [8, 4, 2, 64], P('gx', 'gy'), may hold values from 0 to 255
- send_diag: int32 [8, 4, 2, 32], P('gx', 'gy'), may hold values from 0 to 255
- depart_tile: int32 [8, 4, 2, 256], P('gx', 'gy'), may hold values from 0 to 5, as said below
- depart_slot: int32 [8, 4, 2, 256], P('gx', 'gy'), may hold values from 0 to 255, as said below
- interp_weights: bfloat16 [8, 4, 256, 64, 128], P('gx', 'gy'), may hold values from 0 to 1, as said below
Outputs:
- pair_next: float32 [8, 4, 256, 128], P('gx', 'gy')
Inputs may be any that keep to these rules, and one draw needn't show every extreme that they name: `depart_tile`: 0 is the own tile, 1 the upstream tile along gx, 2 the spanwise neighbour at lower gy, 3 the one at higher gy, 4 and 5 the upstream tile's neighbours at lower and higher gy. `depart_slot`: below 256 for tile 0, 128 for tile 1, 64 for tiles 2 and 3, 32 for tiles 4 and 5; each bound minus one is reached. `interp_weights`: the 128 columns are the cells of the two departure blocks taken as a 4 x 4 x 8 box; each cell's row holds the eight trilinear weights of one point inside that box, summing to one, and zeros elsewhere.
All inputs are finite; a program needn't handle non-finite values.
Results may differ from a plain program's by a relative error of at most 0.0003.
Values sent between devices are 32-bit elements; how exact they have to be, the bound alone decides.
No kernel may reach another device: no remote copies, remote signals or barrier semaphores. Data moves between devices by JAX's collectives and lax.ppermute only.
A program may use at most 64 MiB of HBM per device.

v0:
```python
import jax
import jax.numpy as jnp
from jax import lax
from jax.sharding import PartitionSpec as P

NBD = 256
CAPX = 128
CAPY = 64
CAPD = 32


time_step = 0.5


def with_halo(cells, sides, width):
    for axis, dim in sides:
        count = lax.axis_size(axis)
        head = lax.slice_in_dim(cells, 0, width, axis=dim)
        tail = lax.slice_in_dim(cells, cells.shape[dim] - width, cells.shape[dim], axis=dim)
        cells = jnp.concatenate(
            [
                lax.ppermute(tail, axis, [(i, (i + 1) % count) for i in range(count)]),
                cells,
                lax.ppermute(head, axis, [((i + 1) % count, i) for i in range(count)]),
            ],
            axis=dim,
        )
    return cells


def from_behind(block, axis, distance):
    devices = range(lax.axis_size(axis))
    route = [((i - distance) % len(devices), i) for i in devices]
    return lax.ppermute(block, axis, route)


def vertical_diff(field):
    return jnp.concatenate(
        [
            field[:, :, 1:2] - field[:, :, 0:1],
            (field[:, :, 2:] - field[:, :, :-2]) * 0.5,
            field[:, :, -1:] - field[:, :, -2:-1],
        ],
        axis=2,
    )


def strain_parts(field):
    along_x = (field[:, 2:, :, 1:-1] - field[:, :-2, :, 1:-1]) * 0.5
    along_y = (field[:, 1:-1, :, 2:] - field[:, 1:-1, :, :-2]) * 0.5
    along_z = vertical_diff(field[:, 1:-1, :, 1:-1])
    gradient = jnp.stack([along_x, along_y, along_z], axis=1)
    strain_rate = 0.5 * (gradient + jnp.swapaxes(gradient, 0, 1))
    magnitude = jnp.sqrt(2.0 * jnp.sum(strain_rate * strain_rate, axis=(0, 1)))
    return (strain_rate, magnitude)


def test_filter(field):
    across = (
        0.25 * field[..., :-2, :, :] + 0.5 * field[..., 1:-1, :, :] + 0.25 * field[..., 2:, :, :]
    )
    return 0.25 * across[..., :-2] + 0.5 * across[..., 1:-1] + 0.25 * across[..., 2:]


def model_terms(extended):
    strain_rate, magnitude = strain_parts(extended)
    filtered_product = test_filter(magnitude * strain_rate)
    smooth = test_filter(extended)
    strain_test, magnitude_test = strain_parts(smooth)
    model_tensor = 2.0 * (filtered_product - 4.0 * magnitude_test * strain_test)
    center = extended[:, 1:-1, :, 1:-1]
    smooth_center = smooth[:, 1:-1, :, 1:-1]
    leonard = (
        test_filter(center[:, None] * center[None, :])
        - smooth_center[:, None] * smooth_center[None, :]
    )
    return (
        jnp.sum(leonard * model_tensor, axis=(0, 1)),
        jnp.sum(model_tensor * model_tensor, axis=(0, 1)),
    )


def slot_offsets(tile_ids):
    starts = jnp.array(
        [
            0,
            NBD,
            NBD + CAPX,
            NBD + CAPX + CAPY,
            NBD + CAPX + 2 * CAPY,
            NBD + CAPX + 2 * CAPY + CAPD,
        ],
        jnp.int32,
    )
    match = tile_ids[..., None] == jnp.arange(6, dtype=jnp.int32)
    return jnp.sum(jnp.where(match, starts, 0), axis=-1)


def departure_update(weights, first, second, lm_blocks, mm_blocks):
    lm_rows = jnp.concatenate([first[..., :64], second[..., :64]], axis=-1)
    mm_rows = jnp.concatenate([first[..., 64:], second[..., 64:]], axis=-1)
    stacked = jnp.stack([lm_rows, mm_rows], axis=-2)
    departed = jnp.einsum(
        "...kij,...kcj->...kci",
        weights.astype(jnp.float32),
        stacked,
        precision=lax.Precision.HIGHEST,
    )
    lm_depart = departed[..., 0, :]
    mm_depart = departed[..., 1, :]
    timescale = 1.5 * (lm_depart * mm_depart) ** (-0.125)
    ratio = time_step / timescale
    weight_new = ratio / (1.0 + ratio)
    lm_next = jnp.maximum(weight_new * lm_blocks + (1.0 - weight_new) * lm_depart, 0.0)
    mm_next = weight_new * mm_blocks + (1.0 - weight_new) * mm_depart
    return jnp.concatenate([lm_next, mm_next], axis=-1)


def on_device(
    velocity, pair_blocks, send_up, send_side, send_diag, depart_tile, depart_slot, interp_weights
):
    extended = with_halo(velocity, (("gx", 1), ("gy", 3)), 2)
    lm_field, mm_field = model_terms(extended)
    lm_blocks = lm_field.reshape(NBD, 64)
    mm_blocks = mm_field.reshape(NBD, 64)
    own_rows = pair_blocks[0, 0]
    upper_rows, upper_list, upper_diag = from_behind(
        (own_rows, send_up[0, 0], send_diag[0, 0]), "gx", 1
    )
    from_up = upper_rows[upper_list]
    low_rows, low_side, low_corner, low_corner_list = from_behind(
        (own_rows, send_side[0, 0], upper_rows, upper_diag), "gy", 1
    )
    from_low = low_rows[low_side[0]]
    diag_low = low_corner[low_corner_list[0]]
    high_rows, high_side, high_corner, high_corner_list = from_behind(
        (own_rows, send_side[0, 0], upper_rows, upper_diag), "gy", -1
    )
    from_high = high_rows[high_side[1]]
    diag_high = high_corner[high_corner_list[1]]
    candidates = jnp.concatenate(
        [own_rows, from_up, from_low, from_high, diag_low, diag_high], axis=0
    )
    pool_index = slot_offsets(depart_tile[0, 0]) + depart_slot[0, 0]
    first = candidates[pool_index[0]]
    second = candidates[pool_index[1]]
    result = departure_update(interp_weights[0, 0], first, second, lm_blocks, mm_blocks)
    return result[None, None]


def solution(mesh):
    return jax.shard_map(
        on_device,
        mesh=mesh,
        in_specs=(
            P(None, "gx", None, "gy"),
            P("gx", "gy", None, None),
            P("gx", "gy", None),
            P("gx", "gy", None, None),
            P("gx", "gy", None, None),
            P("gx", "gy", None, None),
            P("gx", "gy", None, None),
            P("gx", "gy", None, None, None),
        ),
        out_specs=P("gx", "gy", None, None),
        check_vma=False,
    )
```

profile of v0, /device:TPU:1, one launch (start us, length us, event | category | flops | bytes accessed | tf_op | source)
XLA Modules:
  0.0 63.4 jit_solution(14884858432643030247)
XLA Ops:
  0.0 2.0 %collective-permute-start = (f32[256,128]{1,0:T(8,128)}, f32[256,128]{1,0:T(8,128)S(1)}, u32[]{:S(2)}, u32[]{:S(2)}) collective-permute-start(f32[256,128]{1,0:T(8,128)} %bitcast.77), channel_id=1, source_target_pairs={{28,0},{0,4},{4,8},{8,12},{12,16},{16,20},{20,24},{24,28},{29,1},{... | collective-permute-start | bytes 393224 | tf_op jit(solution)/shard_map/ppermute | solution.py:34
  2.0 2.1 %collective-permute-start.2 = (f32[256,128]{1,0:T(8,128)}, f32[256,128]{1,0:T(8,128)S(1)}, u32[]{:S(2)}, u32[]{:S(2)}) collective-permute-start(f32[256,128]{1,0:T(8,128)} %bitcast.78), channel_id=1, source_target_pairs={{3,0},{0,1},{1,2},{2,3},{7,4},{4,5},{5,6},{6,7},{11,8},{8,9},{9,10... | collective-permute-start | bytes 393224 | tf_op jit(solution)/shard_map/ppermute | solution.py:34
  4.1 1.3 %collective-permute-start.1 = (s32[128]{0:T(128)}, s32[128]{0:T(128)S(1)}, u32[]{:S(2)}, u32[]{:S(2)}) collective-permute-start(s32[128]{0:T(128)} %bitcast.86), channel_id=1, source_target_pairs={{28,0},{0,4},{4,8},{8,12},{12,16},{16,20},{20,24},{24,28},{29,1},{... | collective-permute-start | bytes 1544 | tf_op jit(solution)/shard_map/ppermute | solution.py:34
  5.4 2.0 %collective-permute-start.3 = (s32[2,64]{1,0:T(2,128)}, s32[2,64]{1,0:T(2,128)S(1)}, u32[]{:S(2)}, u32[]{:S(2)}) collective-permute-start(s32[2,64]{1,0:T(2,128)} %bitcast.84), channel_id=1, source_target_pairs={{3,0},{0,1},{1,2},{2,3},{7,4},{4,5},{5,6},{6,7},{11,8},{8,9},{9,10... | collective-permute-start | bytes 1544 | tf_op jit(solution)/shard_map/ppermute | solution.py:34
  7.4 0.9 %constant_dynamic-update-slice_fusion.5 = f32[576,128]{1,0:T(8,128)S(1)} fusion(f32[1,1,256,128]{3,2,1,0:T(8,128)} %param.10), kind=kLoop, calls=%fused_computation.95 | loop fusion | bytes 262144
  8.3 0.7 %fusion.44 = (f32[3,2,4,128]{3,2,1,0:T(4,128)S(1)}, f32[3,2,4,128]{3,2,1,0:T(4,128)S(1)}) fusion(f32[3,32,4,128]{3,2,1,0:T(4,128)} %param.9), kind=kLoop, calls=%fused_computation.126 | loop fusion | bytes 49152 | tf_op jit(solution)/shard_map/slice | solution.py:18
  9.1 0.8 %fusion.34 = s32[2,256]{1,0:T(2,128)S(1)} fusion(s32[6]{0:T(128)} %constant.21.clone, s32[2,256]{1,0:T(2,128)} %bitcast.82), kind=kLoop, calls=%fused_computation.99 | loop fusion | flops 8704 | bytes 4120 | tf_op jit(solution)/shard_map/reduce_sum | solution.py:96
  9.8 0.7 %bitcast_add_fusion.2 = s32[2,256]{1,0:T(2,128)S(1)} fusion(s32[2,256]{1,0:T(2,128)S(1)} %fusion.34, s32[1,1,2,256]{3,2,1,0:T(2,128)} %param.15), kind=kLoop, calls=%fused_computation.114 | loop fusion | flops 512 | bytes 6144 | tf_op jit(solution)/shard_map/add | solution.py:144
  10.6 0.6 collective-permute-start.5
  11.1 0.8 %collective-permute-start.7 = (s32[2,32]{1,0:T(2,128)}, s32[2,32]{1,0:T(2,128)S(1)}, u32[]{:S(2)}, u32[]{:S(2)}) collective-permute-start(s32[2,32]{1,0:T(2,128)} %bitcast.83), channel_id=1, source_target_pairs={{28,0},{0,4},{4,8},{8,12},{12,16},{16,20},{20,24},{24,28},{29,1},{... | collective-permute-start | bytes 776 | tf_op jit(solution)/shard_map/ppermute | solution.py:34
  11.9 4.5 %collective-permute-done.7 = s32[2,32]{1,0:T(2,128)S(1)} collective-permute-done((s32[2,32]{1,0:T(2,128)}, s32[2,32]{1,0:T(2,128)S(1)}, u32[]{:S(2)}, u32[]{:S(2)}) %collective-permute-start.7) | collective-permute-done | bytes 288 | tf_op jit(solution)/shard_map/ppermute | solution.py:34
  16.5 2.4 %collective-permute-start.8 = (s32[2,32]{1,0:T(2,128)S(1)}, s32[2,32]{1,0:T(2,128)S(1)}, u32[]{:S(2)}, u32[]{:S(2)}) collective-permute-start(s32[2,32]{1,0:T(2,128)S(1)} %collective-permute-done.7), channel_id=1, source_target_pairs={{3,0},{0,1},{1,2},{2,3},{7,4},{4,5},{5,6},{6,7},{11,8},{8,9},{9,10... | collective-permute-start | bytes 776 | tf_op jit(solution)/shard_map/ppermute | solution.py:34
  18.9 0.7 %collective-permute-done.8 = s32[2,32]{1,0:T(2,128)S(1)} collective-permute-done((s32[2,32]{1,0:T(2,128)S(1)}, s32[2,32]{1,0:T(2,128)S(1)}, u32[]{:S(2)}, u32[]{:S(2)}) %collective-permute-start.8) | collective-permute-done | bytes 288 | tf_op jit(solution)/shard_map/ppermute | solution.py:34
  19.6 1.1 %collective-permute-start.10 = (s32[2,32]{1,0:T(2,128)S(1)}, s32[2,32]{1,0:T(2,128)S(1)}, u32[]{:S(2)}, u32[]{:S(2)}) collective-permute-start(s32[2,32]{1,0:T(2,128)S(1)} %collective-permute-done.7), channel_id=1, source_target_pairs={{1,0},{2,1},{3,2},{0,3},{5,4},{6,5},{7,6},{4,7},{9,8},{10,9},{11,1... | collective-permute-start | bytes 776 | tf_op jit(solution)/shard_map/ppermute | solution.py:34
  20.8 2.7 %collective-permute-done.10 = s32[2,32]{1,0:T(2,128)S(1)} collective-permute-done((s32[2,32]{1,0:T(2,128)S(1)}, s32[2,32]{1,0:T(2,128)S(1)}, u32[]{:S(2)}, u32[]{:S(2)}) %collective-permute-start.10) | collective-permute-done | bytes 288 | tf_op jit(solution)/shard_map/ppermute | solution.py:34
  23.4 4.1 %collective-permute-start.12 = (f32[3,2,4,128]{3,2,1,0:T(4,128)S(1)}, f32[3,2,4,128]{3,2,1,0:T(4,128)S(1)}, u32[]{:S(2)}, u32[]{:S(2)}) collective-permute-start(f32[3,2,4,128]{3,2,1,0:T(4,128)S(1)} %get-tuple-element.22), channel_id=1, source_target_pairs={{4,0},{8,4},{12,8},{16,12},{20,16},{24,20},{28,24},{0,28},{5,1},{9... | collective-permute-start | bytes 36872 | tf_op jit(solution)/shard_map/ppermute | solution.py:24
  27.6 1.0 %constant_dynamic-update-slice_fusion.7 = f32[3,36,4,128]{3,2,1,0:T(4,128)S(1)} fusion(f32[3,36,4,128]{3,2,1,0:T(4,128)S(1)} %constant_dynamic-update-slice_fusion.8, f32[3,32,4,128]{3,2,1,0:T(4,128)} %param.9), kind=kLoop, calls=%fused_computation.97 | loop fusion | bytes 393216
  28.8 0.8 %collective-permute-start.13 = (f32[3,36,4,2]{3,2,1,0:T(4,128)S(1)}, f32[3,36,4,2]{3,2,1,0:T(4,128)S(1)}, u32[]{:S(2)}, u32[]{:S(2)}) collective-permute-start(f32[3,36,4,2]{3,2,1,0:T(4,128)S(1)} %get-tuple-element.20), channel_id=1, source_target_pairs={{0,1},{1,2},{2,3},{3,0},{4,5},{5,6},{6,7},{7,4},{8,9},{9,10},{10,1... | collective-permute-start | bytes 10376 | tf_op jit(solution)/shard_map/ppermute | solution.py:22
  29.6 4.5 %collective-permute-done.13 = f32[3,36,4,2]{3,2,1,0:T(4,128)S(1)} collective-permute-done((f32[3,36,4,2]{3,2,1,0:T(4,128)S(1)}, f32[3,36,4,2]{3,2,1,0:T(4,128)S(1)}, u32[]{:S(2)}, u32[]{:S(2)}) %collective-permute-start.13) | collective-permute-done | bytes 3488 | tf_op jit(solution)/shard_map/ppermute | solution.py:22
  34.0 1.4 %collective-permute-done.14 = f32[3,36,4,2]{3,2,1,0:T(4,128)S(1)} collective-permute-done((f32[3,36,4,2]{3,2,1,0:T(4,128)S(1)}, f32[3,36,4,2]{3,2,1,0:T(4,128)S(1)}, u32[]{:S(2)}, u32[]{:S(2)}) %collective-permute-start.14) | collective-permute-done | bytes 3488 | tf_op jit(solution)/shard_map/ppermute | solution.py:24
  35.5 0.4 pad_maximum_fusion.2
  35.9 0.9 %slice_subtract_fusion.5 = (f32[3,34,1,130]{3,2,1,0:T(1,128)S(1)}, f32[3,34,1,130]{3,2,1,0:T(1,128)S(1)}) fusion(f32[3,36,4,132]{3,2,1,0:T(4,128)S(1)} %pad_maximum_fusion.2), kind=kLoop, calls=%fused_computation.83 | loop fusion | flops 26520 | bytes 318240 | tf_op jit(solution)/shard_map/sub | solution.py:40
  36.8 0.5 fusion.28
  37.3 0.7 %fusion.40 = (f32[3,34,4,130]{3,2,1,0:T(4,128)S(1)}, f32[3,1,34,4,130]{4,3,2,0,1:T(4,128)S(1)}) fusion(f32[3,36,4,132]{3,2,1,0:T(4,128)S(1)} %pad_maximum_fusion.2), kind=kLoop, calls=%fused_computation.122 | loop fusion | flops 106080 | bytes 1060800 | tf_op jit(solution)/shard_map/slice | solution.py:71
  38.2 0.5 fusion.21
  38.7 0.5 slice_subtract_fusion.8
  39.1 0.3 fusion.33
  39.4 0.5 fusion.41
  39.9 0.3 maximum_bitcast_fusion
  40.2 0.3 fusion.18
  40.5 0.5 pad_maximum_fusion
  41.0 0.4 multiply_reduce_fusion
  41.8 0.3 fusion.2
  42.1 0.3 fusion.4
  43.0 1.3 %fusion.15 = (f32[32,4,128]{2,1,0:T(4,128)S(1)}, f32[32,4,128]{2,1,0:T(4,128)S(1)}) fusion(f32[3,3,32,4,130]{4,3,2,0,1:T(4,128)S(1)} %fusion.4, f32[3,32,4,128]{3,2,1,0:T(4,128)S(1)} %get-tuple-element.11, f32[32,4,128]{2,1,0:T(4,128)S(1)} %sqrt_multiply_fusion.1, f32[3,3,32,4,128]{4,3,2,1,0:T(4,128)S(1)} %pad_maximum_fusion.1, ...), kind=kLoop, calls=%fused_computation.42 | loop fusion | flops 2916352 | bytes 4718592 | tf_op jit(solution)/shard_map/reduce_sum | solution.py:78
  44.5 0.6 %gather_fusion = f32[128,128]{1,0:T(8,128)S(1)} fusion(f32[256,128]{1,0:T(8,128)S(1)} %collective-permute-done, s32[1024]{0:T(1024)S(1)} %pad_clamp_fusion.6), kind=kCustom, calls=%fused_computation | custom fusion | bytes 131584 | tf_op jit(solution)/shard_map/gather | solution.py:130
  45.2 1.1 %collective-permute-start.6 = (f32[256,128]{1,0:T(8,128)S(1)}, f32[256,128]{1,0:T(8,128)S(1)}, u32[]{:S(2)}, u32[]{:S(2)}) collective-permute-start(f32[256,128]{1,0:T(8,128)S(1)} %collective-permute-done), channel_id=1, source_target_pairs={{3,0},{0,1},{1,2},{2,3},{7,4},{4,5},{5,6},{6,7},{11,8},{8,9},{9,10... | collective-permute-start | bytes 393224 | tf_op jit(solution)/shard_map/ppermute | solution.py:34
  46.3 0.6 gather_fusion.1
  46.9 0.2 collective-permute-start.9
  47.1 0.6 gather_fusion.2
  47.7 0.5 collective-permute-done.6
  48.2 0.6 gather_fusion.3
  48.8 2.7 %collective-permute-done.9 = f32[256,128]{1,0:T(8,128)S(1)} collective-permute-done((f32[256,128]{1,0:T(8,128)S(1)}, f32[256,128]{1,0:T(8,128)S(1)}, u32[]{:S(2)}, u32[]{:S(2)}) %collective-permute-start.9) | collective-permute-done | bytes 131104 | tf_op jit(solution)/shard_map/ppermute | solution.py:34
  51.5 0.6 gather_fusion.4
  52.1 0.7 %gather_fusion.5 = f32[256,128]{1,0:T(8,128)S(1)} fusion(f32[576,128]{1,0:T(8,128)S(1)} %constant_dynamic-update-slice_fusion, s32[1024]{0:T(1024)S(1)} %get-tuple-element.31), kind=kCustom, calls=%fused_computation.5 | custom fusion | bytes 263168 | tf_op jit(solution)/shard_map/gather | solution.py:145
  52.9 0.7 %gather_fusion.6 = f32[256,128]{1,0:T(8,128)S(1)} fusion(f32[576,128]{1,0:T(8,128)S(1)} %constant_dynamic-update-slice_fusion, s32[1024]{0:T(1024)S(1)} %get-tuple-element.30), kind=kCustom, calls=%fused_computation.6 | custom fusion | bytes 263168 | tf_op jit(solution)/shard_map/gather | solution.py:146
  54.0 8.3 %fusion = f32[256,2,64]{2,1,0:T(2,128)S(1)} fusion(bf16[1,1,256,64,128]{4,3,2,1,0:T(8,128)(2,1)} %param.16, f32[256,1,128]{2,1,0:T(1,128)S(1)} %bitcast.74, f32[256,1,128]{2,1,0:T(1,128)S(1)} %bitcast.73), kind=kOutput, calls=%fused_computation.7 | convolution fusion | flops 50397184 | bytes 4587520 | tf_op jit(solution)/shard_map/...kij,...kcj->...kci/dot_general | solution.py:103
  62.7 0.8 %maximum_bitcast_fusion.2 = f32[1,1,256,128]{3,2,1,0:T(8,128)} fusion(f32[256,64]{1,0:T(8,128)S(1)} %get-tuple-element.17, f32[256,64]{1,0:T(8,128)S(1)} %get-tuple-element.16), kind=kLoop, calls=%fused_computation.78 | loop fusion | flops 32768 | bytes 262144 | tf_op jit(solution)/shard_map/broadcast_in_dim | solution.py:148
  (46 shorter events, 2.2 us)
Async XLA Ops:
  0.0 44.5 %collective-permute-start = (f32[256,128]{1,0:T(8,128)}, f32[256,128]{1,0:T(8,128)S(1)}, u32[]{:S(2)}, u32[]{:S(2)}) collective-permute-start(f32[256,128]{1,0:T(8,128)} %bitcast.77), channel_id=1, source_target_pairs={{28,0},{0,4},{4,8},{8,12},{12,16},{16,20},{20,24},{24,28},{29,1},{... | collective-permute-start | bytes 393224 | tf_op jit(solution)/shard_map/ppermute | solution.py:34
  2.0 44.2 %collective-permute-start.2 = (f32[256,128]{1,0:T(8,128)}, f32[256,128]{1,0:T(8,128)S(1)}, u32[]{:S(2)}, u32[]{:S(2)}) collective-permute-start(f32[256,128]{1,0:T(8,128)} %bitcast.78), channel_id=1, source_target_pairs={{3,0},{0,1},{1,2},{2,3},{7,4},{4,5},{5,6},{6,7},{11,8},{8,9},{9,10... | collective-permute-start | bytes 393224 | tf_op jit(solution)/shard_map/ppermute | solution.py:34
  4.1 43.0 %collective-permute-start.4 = (f32[256,128]{1,0:T(8,128)}, f32[256,128]{1,0:T(8,128)S(1)}, u32[]{:S(2)}, u32[]{:S(2)}) collective-permute-start(f32[256,128]{1,0:T(8,128)} %bitcast.79), channel_id=1, source_target_pairs={{1,0},{2,1},{3,2},{0,3},{5,4},{6,5},{7,6},{4,7},{9,8},{10,9},{11,1... | collective-permute-start | bytes 393224 | tf_op jit(solution)/shard_map/ppermute | solution.py:34
  4.1 6.4 %collective-permute-start.1 = (s32[128]{0:T(128)}, s32[128]{0:T(128)S(1)}, u32[]{:S(2)}, u32[]{:S(2)}) collective-permute-start(s32[128]{0:T(128)} %bitcast.86), channel_id=1, source_target_pairs={{28,0},{0,4},{4,8},{8,12},{12,16},{16,20},{20,24},{24,28},{29,1},{... | collective-permute-start | bytes 1544 | tf_op jit(solution)/shard_map/ppermute | solution.py:34
  5.4 5.7 %collective-permute-start.3 = (s32[2,64]{1,0:T(2,128)}, s32[2,64]{1,0:T(2,128)S(1)}, u32[]{:S(2)}, u32[]{:S(2)}) collective-permute-start(s32[2,64]{1,0:T(2,128)} %bitcast.84), channel_id=1, source_target_pairs={{3,0},{0,1},{1,2},{2,3},{7,4},{4,5},{5,6},{6,7},{11,8},{8,9},{9,10... | collective-permute-start | bytes 1544 | tf_op jit(solution)/shard_map/ppermute | solution.py:34
  10.6 5.9 %collective-permute-start.5 = (s32[2,64]{1,0:T(2,128)}, s32[2,64]{1,0:T(2,128)S(1)}, u32[]{:S(2)}, u32[]{:S(2)}) collective-permute-start(s32[2,64]{1,0:T(2,128)} %bitcast.85), channel_id=1, source_target_pairs={{1,0},{2,1},{3,2},{0,3},{5,4},{6,5},{7,6},{4,7},{9,8},{10,9},{11,1... | collective-permute-start | bytes 1544 | tf_op jit(solution)/shard_map/ppermute | solution.py:34
  11.1 5.3 %collective-permute-start.7 = (s32[2,32]{1,0:T(2,128)}, s32[2,32]{1,0:T(2,128)S(1)}, u32[]{:S(2)}, u32[]{:S(2)}) collective-permute-start(s32[2,32]{1,0:T(2,128)} %bitcast.83), channel_id=1, source_target_pairs={{28,0},{0,4},{4,8},{8,12},{12,16},{16,20},{20,24},{24,28},{29,1},{... | collective-permute-start | bytes 776 | tf_op jit(solution)/shard_map/ppermute | solution.py:34
  16.5 11.1 %collective-permute-start.11 = (f32[3,2,4,128]{3,2,1,0:T(4,128)S(1)}, f32[3,2,4,128]{3,2,1,0:T(4,128)S(1)}, u32[]{:S(2)}, u32[]{:S(2)}) collective-permute-start(f32[3,2,4,128]{3,2,1,0:T(4,128)S(1)} %get-tuple-element.23), channel_id=1, source_target_pairs={{0,4},{4,8},{8,12},{12,16},{16,20},{20,24},{24,28},{28,0},{1,5},{5... | collective-permute-start | bytes 36872 | tf_op jit(solution)/shard_map/ppermute | solution.py:22
  16.5 3.2 %collective-permute-start.8 = (s32[2,32]{1,0:T(2,128)S(1)}, s32[2,32]{1,0:T(2,128)S(1)}, u32[]{:S(2)}, u32[]{:S(2)}) collective-permute-start(s32[2,32]{1,0:T(2,128)S(1)} %collective-permute-done.7), channel_id=1, source_target_pairs={{3,0},{0,1},{1,2},{2,3},{7,4},{4,5},{5,6},{6,7},{11,8},{8,9},{9,10... | collective-permute-start | bytes 776 | tf_op jit(solution)/shard_map/ppermute | solution.py:34
  19.6 3.8 %collective-permute-start.10 = (s32[2,32]{1,0:T(2,128)S(1)}, s32[2,32]{1,0:T(2,128)S(1)}, u32[]{:S(2)}, u32[]{:S(2)}) collective-permute-start(s32[2,32]{1,0:T(2,128)S(1)} %collective-permute-done.7), channel_id=1, source_target_pairs={{1,0},{2,1},{3,2},{0,3},{5,4},{6,5},{7,6},{4,7},{9,8},{10,9},{11,1... | collective-permute-start | bytes 776 | tf_op jit(solution)/shard_map/ppermute | solution.py:34
  23.4 5.1 %collective-permute-start.12 = (f32[3,2,4,128]{3,2,1,0:T(4,128)S(1)}, f32[3,2,4,128]{3,2,1,0:T(4,128)S(1)}, u32[]{:S(2)}, u32[]{:S(2)}) collective-permute-start(f32[3,2,4,128]{3,2,1,0:T(4,128)S(1)} %get-tuple-element.22), channel_id=1, source_target_pairs={{4,0},{8,4},{12,8},{16,12},{20,16},{24,20},{28,24},{0,28},{5,1},{9... | collective-permute-start | bytes 36872 | tf_op jit(solution)/shard_map/ppermute | solution.py:24
  28.8 5.2 %collective-permute-start.13 = (f32[3,36,4,2]{3,2,1,0:T(4,128)S(1)}, f32[3,36,4,2]{3,2,1,0:T(4,128)S(1)}, u32[]{:S(2)}, u32[]{:S(2)}) collective-permute-start(f32[3,36,4,2]{3,2,1,0:T(4,128)S(1)} %get-tuple-element.20), channel_id=1, source_target_pairs={{0,1},{1,2},{2,3},{3,0},{4,5},{5,6},{6,7},{7,4},{8,9},{9,10},{10,1... | collective-permute-start | bytes 10376 | tf_op jit(solution)/shard_map/ppermute | solution.py:22
  29.6 5.9 %collective-permute-start.14 = (f32[3,36,4,2]{3,2,1,0:T(4,128)S(1)}, f32[3,36,4,2]{3,2,1,0:T(4,128)S(1)}, u32[]{:S(2)}, u32[]{:S(2)}) collective-permute-start(f32[3,36,4,2]{3,2,1,0:T(4,128)S(1)} %get-tuple-element.21), channel_id=1, source_target_pairs={{1,0},{2,1},{3,2},{0,3},{5,4},{6,5},{7,6},{4,7},{9,8},{10,9},{11,1... | collective-permute-start | bytes 10376 | tf_op jit(solution)/shard_map/ppermute | solution.py:24
  45.2 3.0 %collective-permute-start.6 = (f32[256,128]{1,0:T(8,128)S(1)}, f32[256,128]{1,0:T(8,128)S(1)}, u32[]{:S(2)}, u32[]{:S(2)}) collective-permute-start(f32[256,128]{1,0:T(8,128)S(1)} %collective-permute-done), channel_id=1, source_target_pairs={{3,0},{0,1},{1,2},{2,3},{7,4},{4,5},{5,6},{6,7},{11,8},{8,9},{9,10... | collective-permute-start | bytes 393224 | tf_op jit(solution)/shard_map/ppermute | solution.py:34
  46.9 4.6 %collective-permute-start.9 = (f32[256,128]{1,0:T(8,128)S(1)}, f32[256,128]{1,0:T(8,128)S(1)}, u32[]{:S(2)}, u32[]{:S(2)}) collective-permute-start(f32[256,128]{1,0:T(8,128)S(1)} %collective-permute-done), channel_id=1, source_target_pairs={{1,0},{2,1},{3,2},{0,3},{5,4},{6,5},{7,6},{4,7},{9,8},{10,9},{11,1... | collective-permute-start | bytes 393224 | tf_op jit(solution)/shard_map/ppermute | solution.py:34
where the time goes:
time: 63.7 us; the launch traced here: 63.4 us
  starting transfers between devices  18.6 us (29%)
  waiting for transfers between devices  17 us (27%)
  other arithmetic  11.4 us (18%)
  matrix products  8.3 us (13%)
  local copies, waits for them, and re-layouts  7.88 us (12%)
    ppermute x11, starting transfers between devices, from_behind(): return lax.ppermute(block, axis, route)  13.7 us
    ppermute x11, waiting for transfers between devices, from_behind(): return lax.ppermute(block, axis, route)  11.1 us
    dot_general x1, matrix products, departure_update(): jnp.einsum('...kij,...kcj->...kci', weights.astype(jnp.float32), stacked,...  8.3 us
    ppermute x2, waiting for transfers between devices, with_halo(): lax.ppermute(tail, axis, [(i, (i + 1) % count) for i in range(count)])  4.46 us
    ppermute x2, starting transfers between devices, with_halo(): lax.ppermute(head, axis, [((i + 1) % count, i) for i in range(count)])  4.15 us
    unnamed x7, local copies, waits for them, and re-layouts  1.89 us
    ppermute x2, waiting for transfers between devices, with_halo(): lax.ppermute(head, axis, [((i + 1) % count, i) for i in range(count)])  1.45 us
    another operation x5, other arithmetic, strain_parts(): gradient = jnp.stack([along_x, along_y, along_z], axis=1)  1.42 us
  transfers between devices with their start and end apart: 15, of which 7 were waited for; matrix products, arithmetic and copies ran while one was open for 25% of the time, Pallas kernels for 0%

commit v1 on v0

v1 whole, which is shorter than its diff:
```python
import functools

import jax
import jax.numpy as jnp
from jax import lax
from jax.experimental import pallas as pl
from jax.experimental.pallas import tpu as pltpu
from jax.sharding import PartitionSpec as P

CX = 32
LZ = 4
NBD = 256
CAPX = 128
CAPY = 64
CAPD = 32

TIME_STEP = 0.5

VEL_AT = CAPD
DIAG1_AT = CAPD + 24
UP_AT = 2 * CAPD + 24
X_ROWS = UP_AT + CAPX
Y_ROWS = CAPY + CX
R_ROWS = CAPD + 8

POOL = NBD + CAPX + 2 * CAPY + 2 * CAPD
POOL_PAD = 640
UP_POOL = NBD
LOW_POOL = NBD + CAPX
HIGH_POOL = LOW_POOL + CAPY
DIAG_LOW_POOL = HIGH_POOL + CAPY
DIAG_HIGH_POOL = DIAG_LOW_POOL + CAPD

EXT = 48
F32 = jnp.float32
BF16 = jnp.bfloat16


def lanes_of(shape):
    return lax.broadcasted_iota(jnp.int32, shape, 1)


def roll_lanes(x, shift):
    shift = shift % 128
    return x if shift == 0 else pltpu.roll(x, shift, 1)


def odd(axis):
    return lax.rem(lax.axis_index(axis), 2) == 1


def pack_x_kernel(up_list, diag_list, rows, vel, s0, t0):
    is_odd = odd("gx")

    def gather(out):
        for i in range(CAPD):
            out[i : i + 1, :] = rows[pl.ds(diag_list[0, i], 1), :]
            out[DIAG1_AT + i : DIAG1_AT + i + 1, :] = rows[pl.ds(diag_list[1, i], 1), :]
        for i in range(CAPX):
            out[UP_AT + i : UP_AT + i + 1, :] = rows[pl.ds(up_list[i], 1), :]

    def edge(out, at):
        for c in range(3):
            out[VEL_AT + 8 * c : VEL_AT + 8 * c + 8, :] = vel[c * 128 + at : c * 128 + at + 8, :]

    @pl.when(is_odd)
    def _():
        gather(s0)
        edge(s0, 120)
        edge(t0, 0)

    @pl.when(jnp.logical_not(is_odd))
    def _():
        gather(t0)
        edge(t0, 120)
        edge(s0, 0)


def pack_y_kernel(side_list, rows, vel, y1, y0):
    is_odd = odd("gy")
    first = jnp.where(is_odd, 0, 1)
    for i in range(CAPY):
        y1[i : i + 1, :] = rows[pl.ds(side_list[first, i], 1), :]
        y0[i : i + 1, :] = rows[pl.ds(side_list[1 - first, i], 1), :]
    lane = lanes_of((8, 128))
    for xv in range(4):
        plus = jnp.zeros((8, 128), F32)
        minus = jnp.zeros((8, 128), F32)
        for z in range(LZ):
            for c in range(3):
                base = z * 32 + c * 8
                plane = vel[pl.ds(c * 128 + xv * 32 + z, 8, stride=4), :]
                here = (lane >= base) & (lane < base + 2)
                plus = jnp.where(here, roll_lanes(plane, base - 126), plus)
                minus = jnp.where(here, roll_lanes(plane, base), minus)
        at = CAPY + 8 * xv
        y1[at : at + 8, :] = jnp.where(is_odd, plus, minus)
        y0[at : at + 8, :] = jnp.where(is_odd, minus, plus)


def relay_kernel(s0, t0, ry1, ry0):
    x_odd = odd("gx")
    y_odd = odd("gy")

    def upper(at):
        return jnp.where(x_odd, t0[at : at + 8, :], s0[at : at + 8, :])

    def lower(at):
        return jnp.where(x_odd, s0[at : at + 8, :], t0[at : at + 8, :])

    for i in range(0, CAPD, 8):
        plus, minus = upper(i), upper(DIAG1_AT + i)
        ry1[i : i + 8, :] = jnp.where(y_odd, plus, minus)
        ry0[i : i + 8, :] = jnp.where(y_odd, minus, plus)
    lane = lanes_of((8, 128))
    plus = jnp.zeros((8, 128), F32)
    minus = jnp.zeros((8, 128), F32)
    for c in range(3):
        for k, part in enumerate((upper(VEL_AT + 8 * c), lower(VEL_AT + 8 * c))):
            base = (2 * c + k) * 8
            here = (lane >= base) & (lane < base + 2)
            plus = jnp.where(here, roll_lanes(part, base - 126), plus)
            minus = jnp.where(here, roll_lanes(part, base), minus)
    ry1[CAPD:, :] = jnp.where(y_odd, plus, minus)
    ry0[CAPD:, :] = jnp.where(y_odd, minus, plus)


PAIRS = ((0, 0), (1, 1), (2, 2), (0, 1), (0, 2), (1, 2))


def plane_diff(f):
    last = len(f) - 1
    return [
        f[1] - f[0]
        if p == 0
        else f[last] - f[last - 1]
        if p == last
        else (f[p + 1] - f[p - 1]) * 0.5
        for p in range(last + 1)
    ]


def strip_diff(f):
    (f,) = f
    level = lanes_of(f.shape) // 32
    above, below = roll_lanes(f, -32), roll_lanes(f, 32)
    inner = (above - below) * 0.5
    return [jnp.where(level == 0, above - f, jnp.where(level == LZ - 1, f - below, inner))]


def strain(before, here, after, along_z):
    grad = [
        (
            (after[i] - before[i]) * 0.5,
            (roll_lanes(here[i], -1) - roll_lanes(here[i], 1)) * 0.5,
            along_z[i],
        )
        for i in range(3)
    ]
    rate = [grad[i][j] if i == j else 0.5 * (grad[i][j] + grad[j][i]) for i, j in PAIRS]
    own = rate[0] * rate[0] + rate[1] * rate[1] + rate[2] * rate[2]
    cross = rate[3] * rate[3] + rate[4] * rate[4] + rate[5] * rate[5]
    return rate, jnp.sqrt(2.0 * own + 4.0 * cross)


def filtered(before, here, after):
    across = 0.25 * (before + after) + 0.5 * here
    return 0.25 * (roll_lanes(across, 1) + roll_lanes(across, -1)) + 0.5 * across


def stencil(u, q, planes, diff, emit):
    for r in range(0, CX + 8, 8):
        here = [[u[c, p, r + 1 : r + 9, :] for p in range(planes)] for c in range(3)]
        along_z = [diff(here[c]) for c in range(3)]
        for p in range(planes):
            before = [u[c, p, r : r + 8, :] for c in range(3)]
            after = [u[c, p, r + 2 : r + 10, :] for c in range(3)]
            mid = [here[c][p] for c in range(3)]
            rate, size = strain(before, mid, after, [along_z[c][p] for c in range(3)])
            for n, (i, j) in enumerate(PAIRS):
                q[n, p, r : r + 8, :] = size * rate[n]
                q[6 + n, p, r : r + 8, :] = mid[i] * mid[j]
            for c in range(3):
                q[12 + c, p, r : r + 8, :] = filtered(before[c], mid[c], after[c])
    for r in range(0, CX, 8):
        here = [[q[12 + c, p, r + 1 : r + 9, :] for p in range(planes)] for c in range(3)]
        along_z = [diff(here[c]) for c in range(3)]
        for p in range(planes):
            before = [q[12 + c, p, r : r + 8, :] for c in range(3)]
            after = [q[12 + c, p, r + 2 : r + 10, :] for c in range(3)]
            mid = [here[c][p] for c in range(3)]
            rate, size = strain(before, mid, after, [along_z[c][p] for c in range(3)])
            size = 4.0 * size

            def smoothed(n):
                return filtered(
                    q[n, p, r : r + 8, :], q[n, p, r + 1 : r + 9, :], q[n, p, r + 2 : r + 10, :]
                )

            lm, mm = 0.0, 0.0
            for n, (i, j) in enumerate(PAIRS):
                model = 2.0 * (smoothed(n) - size * rate[n])
                leonard = smoothed(6 + n) - mid[i] * mid[j]
                weight = 1.0 if i == j else 2.0
                lm += weight * (leonard * model)
                mm += weight * (model * model)
            emit(p, r, lm, mm)


def main_kernel(
    vel, s0, t0, y1, y0, tiles, slots, weights, lm, mm, strips, picks, held, u, q, sem
):
    fetch = pltpu.make_async_copy(weights, held, sem)
    fetch.start()
    x_odd, y_odd = odd("gx"), odd("gy")
    lane = lanes_of((8, 128))
    for c in range(3):
        for z in range(LZ):
            at = VEL_AT + 8 * c + z
            s_rows = s0[pl.ds(at, 2, stride=4), :]
            t_rows = t0[pl.ds(at, 2, stride=4), :]
            u[c, z, 0:2, :] = jnp.where(x_odd, t_rows, s_rows)
            u[c, z, 2 : CX + 2, :] = vel[pl.ds(c * 128 + z, CX, stride=4), :]
            u[c, z, CX + 2 : CX + 4, :] = jnp.where(x_odd, s_rows, t_rows)
    for c in range(3):
        for r in range(0, CX + 8, 8):
            strip = jnp.zeros((8, 128), F32)
            for z in range(LZ):
                base = 32 * z
                plane = u[c, z, r : r + 8, :]
                left = (lane >= base + 2) & (lane < base + 6)
                right = (lane >= base + 16) & (lane < base + 20)
                strip = jnp.where(left, roll_lanes(plane, base + 2), strip)
                strip = jnp.where(right, roll_lanes(plane, base + 16 - 124), strip)
            strips[c, r : r + 8, :] = strip
        for r in range(0, CX, 8):
            at = CAPY + r
            low = jnp.where(y_odd, y0[at : at + 8, :], y1[at : at + 8, :])
            high = jnp.where(y_odd, y1[at : at + 8, :], y0[at : at + 8, :])
            strip = strips[c, r + 2 : r + 10, :]
            strip = jnp.where(lane % 32 < 2, roll_lanes(low, -8 * c), strip)
            here = (lane % 32 >= 20) & (lane % 32 < 22)
            strip = jnp.where(here, roll_lanes(high, 20 - 8 * c), strip)
            strips[c, r + 2 : r + 10, :] = strip

    def emit(z, r, lm_part, mm_part):
        for k in range(2):
            lm[pl.ds(8 * r + 2 * z + k, 8, stride=8), :] = lm_part
            mm[pl.ds(8 * r + 2 * z + k, 8, stride=8), :] = mm_part

    stencil(u, q, LZ, plane_diff, emit)

    tile = tiles[...]
    starts = (0, UP_POOL, LOW_POOL, HIGH_POOL, DIAG_LOW_POOL, DIAG_HIGH_POOL)
    index = slots[...]
    for n, start in enumerate(starts):
        index = index + jnp.where(tile == n, start, 0)
    index = index.astype(F32)
    column = lanes_of((128, 128)).astype(F32)
    for k in range(2):
        for half in range(2):
            line = index[k : k + 1, half * 128 : half * 128 + 128]
            wanted = jnp.transpose(jnp.broadcast_to(line, (128, 128)))
            for part in range(POOL_PAD // 128):
                hit = wanted == column + 128.0 * part
                at = k * NBD + half * 128
                picks[at : at + 128, part * 128 : part * 128 + 128] = jnp.where(
                    hit, 1.0, 0.0
                ).astype(BF16)
    fetch.wait()


def final_kernel(
    lm_in, mm_in, strips, ry1, ry0, s0, t0, y1, y0, rows, picks, weights, out,
    u, q, lm, mm, pool, picked,
):
    x_odd, y_odd = odd("gx"), odd("gy")
    lane = lanes_of((8, 128))
    lm[...] = lm_in[...]
    mm[...] = mm_in[...]

    def candidates(at, value):
        high = value.astype(BF16)
        size = value.shape[0]
        pool[at : at + size, 0:128] = high
        pool[at : at + size, 128:256] = (value - high.astype(F32)).astype(BF16)

    candidates(0, rows[...])
    candidates(UP_POOL, jnp.where(x_odd, t0[UP_AT:, :], s0[UP_AT:, :]))
    candidates(LOW_POOL, jnp.where(y_odd, y0[:CAPY, :], y1[:CAPY, :]))
    candidates(HIGH_POOL, jnp.where(y_odd, y1[:CAPY, :], y0[:CAPY, :]))
    candidates(DIAG_LOW_POOL, jnp.where(y_odd, ry0[:CAPD, :], ry1[:CAPD, :]))
    candidates(DIAG_HIGH_POOL, jnp.where(y_odd, ry1[:CAPD, :], ry0[:CAPD, :]))
    pool[POOL:, :] = jnp.zeros((POOL_PAD - POOL, 256), BF16)
    picked[...] = jnp.dot(picks[...], pool[...], preferred_element_type=F32)

    low = jnp.where(y_odd, ry0[CAPD:, :], ry1[CAPD:, :])
    high = jnp.where(y_odd, ry1[CAPD:, :], ry0[CAPD:, :])
    level = lane // 32
    u[...] = strips[...].reshape(u.shape)
    for c in range(3):
        for k, at in enumerate((0, CX + 2)):
            base = (2 * c + k) * 8
            for x in range(2):
                row = u[c, 0, at + x : at + x + 1, :]
                one = lanes_of((1, 128))
                for z in range(LZ):
                    line = low[4 * x + z : 4 * x + z + 1, :]
                    here = (one >= 32 * z) & (one < 32 * z + 2)
                    row = jnp.where(here, roll_lanes(line, 32 * z - base), row)
                    line = high[4 * x + z : 4 * x + z + 1, :]
                    here = (one >= 32 * z + 20) & (one < 32 * z + 22)
                    row = jnp.where(here, roll_lanes(line, 32 * z + 20 - base), row)
                u[c, 0, at + x : at + x + 1, :] = row
    del level

    def emit(_, r, lm_part, mm_part):
        for into, part in ((lm, lm_part), (mm, mm_part)):
            for z in range(LZ):
                left = roll_lanes(part, -(32 * z + 2))
                right = roll_lanes(part, 126 - (32 * z + 18))
                for k in range(2):
                    at = pl.ds(8 * r + 2 * z + k, 8, stride=8)
                    value = jnp.where(lane < 2, left, jnp.where(lane >= 126, right, into[at, :]))
                    into[at, :] = value

    stencil(u, q, 1, strip_diff, emit)

    row_of = lax.broadcasted_iota(jnp.int32, (8, 128), 0)
    front = lane < 64
    even = row_of % 2 == 0
    for x in range(CX):
        terms = []
        for half in range(2):
            first = picked[8 * x : 8 * x + 8, 128 * half : 128 * half + 128]
            second = picked[NBD + 8 * x : NBD + 8 * x + 8, 128 * half : 128 * half + 128]
            terms.append(jnp.where(front, first, roll_lanes(second, 64)))
            terms.append(jnp.where(front, roll_lanes(first, 64), second))
        left = jnp.concatenate(terms, axis=0).astype(BF16)
        product = lax.dot_general(
            left,
            weights[512 * x : 512 * x + 512, :],
            (((1,), (1,)), ((), ())),
            preferred_element_type=F32,
        )
        product = product[:16] + product[16:]
        found = []
        for at in (0, 8):
            merged = product[at : at + 8, 384:512]
            for part in (2, 1, 0):
                mine = row_of // 2 == part
                merged = jnp.where(mine, product[at : at + 8, 128 * part : 128 * part + 128], merged)
            found.append(merged)
        lm_depart, mm_depart = found
        lm_block, mm_block = lm[8 * x : 8 * x + 8, :], mm[8 * x : 8 * x + 8, :]
        ratio = (TIME_STEP / 1.5) * jnp.exp(0.125 * jnp.log(lm_depart * mm_depart))
        weight = ratio / (1.0 + ratio)
        lm_next = jnp.maximum(weight * lm_block + (1.0 - weight) * lm_depart, 0.0)
        mm_next = weight * mm_block + (1.0 - weight) * mm_depart
        lm_next = jnp.where(even, lm_next, roll_lanes(lm_next, 64))
        mm_next = jnp.where(even, roll_lanes(mm_next, 64), mm_next)
        out[8 * x : 8 * x + 8, :] = jnp.where(front, lm_next, mm_next)


def vmem(count=1):
    return [pl.BlockSpec(memory_space=pltpu.VMEM)] * count


def smem(count=1):
    return [pl.BlockSpec(memory_space=pltpu.SMEM)] * count


def array(*shape, dtype=F32):
    return jax.ShapeDtypeStruct(shape, dtype)


def call(kernel, ins, outs, scratch=(), flops=1000):
    return pl.pallas_call(
        kernel,
        in_specs=ins,
        out_specs=tuple(vmem(len(outs))) if isinstance(outs, tuple) else vmem()[0],
        out_shape=outs,
        scratch_shapes=list(scratch),
        compiler_params=pltpu.CompilerParams(vmem_limit_bytes=32 * 1024 * 1024),
        cost_estimate=pl.CostEstimate(flops=flops, bytes_accessed=flops, transcendentals=0),
    )


def swap(block, axis, start):
    count = lax.axis_size(axis)
    ahead = [(i, (i + 1) % count) for i in range(start, count, 2)]
    return lax.ppermute(block, axis, ahead + [(j, i) for i, j in ahead])


def on_device(
    velocity, pair_blocks, send_up, send_side, send_diag, depart_tile, depart_slot, interp_weights
):
    vel = velocity.reshape(3 * CX * LZ, 128)
    rows = pair_blocks[0, 0]
    weights = interp_weights.reshape(NBD * 64, 128)

    s0, t0 = call(pack_x_kernel, smem(2) + vmem(2), (array(X_ROWS, 128),) * 2)(
        send_up[0, 0], send_diag[0, 0], rows, vel
    )
    s0 = swap(s0, "gx", 1)
    t0 = swap(t0, "gx", 0)
    y1, y0 = call(pack_y_kernel, smem(1) + vmem(2), (array(Y_ROWS, 128),) * 2)(
        send_side[0, 0], rows, vel
    )
    y1 = swap(y1, "gy", 1)
    y0 = swap(y0, "gy", 0)
    ry1, ry0 = call(relay_kernel, vmem(2), (array(R_ROWS, 128),) * 2)(s0, t0)
    ry1 = swap(ry1, "gy", 1)
    ry0 = swap(ry0, "gy", 0)
    lm, mm, strips, picks, held = call(
        main_kernel,
        vmem(7) + [pl.BlockSpec(memory_space=pl.ANY)],
        (
            array(NBD, 128),
            array(NBD, 128),
            array(3, EXT, 128),
            array(2 * NBD, POOL_PAD, dtype=BF16),
            array(NBD * 64, 128, dtype=BF16),
        ),
        [
            pltpu.VMEM((3, LZ, EXT, 128), F32),
            pltpu.VMEM((15, LZ, EXT, 128), F32),
            pltpu.SemaphoreType.DMA,
        ],
        flops=4000000,
    )(vel, s0, t0, y1, y0, depart_tile[0, 0], depart_slot[0, 0], weights)
    result = call(
        final_kernel,
        vmem(12),
        array(NBD, 128),
        [
            pltpu.VMEM((3, 1, EXT, 128), F32),
            pltpu.VMEM((15, 1, EXT, 128), F32),
            pltpu.VMEM((NBD, 128), F32),
            pltpu.VMEM((NBD, 128), F32),
            pltpu.VMEM((POOL_PAD, 256), BF16),
            pltpu.VMEM((2 * NBD, 256), F32),
        ],
    )(lm, mm, strips, ry1, ry0, s0, t0, y1, y0, rows, picks, held)
    return result[None, None]


def solution(mesh):
    return jax.shard_map(
        on_device,
        mesh=mesh,
        in_specs=(
            P(None, "gx", None, "gy"),
            P("gx", "gy", None, None),
            P("gx", "gy", None),
            P("gx", "gy", None, None),
            P("gx", "gy", None, None),
            P("gx", "gy", None, None),
            P("gx", "gy", None, None),
            P("gx", "gy", None, None, None),
        ),
        out_specs=P("gx", "gy", None, None),
        check_vma=False,
    )
```

time: 63.7 us -> 26.3 us (0.41)
  the two profiles are of different devices: /device:TPU:1 before, /device:TPU:0 now
where the time goes in v1:
time: 26.3 us; the launch traced here: 25.9 us
  local copies, waits for them, and re-layouts  10.2 us (39%)
  starting transfers between devices  9.4 us (36%)
  Pallas kernels  5.74 us (22%)
  waiting for transfers between devices  0.6 us (2%)
    unnamed x24, local copies, waits for them, and re-layouts  10.2 us
    ppermute x6, starting transfers between devices, swap(): return lax.ppermute(block, axis, ahead + [(j, i) for i, j in ahead])  9.4 us
    pallas_call x1, Pallas kernels, on_device(): call(final_kernel, vmem(12), array(NBD, 128), [pltpu.VMEM((3, 1, EXT, 128...  2.83 us
    pallas_call x1, Pallas kernels, on_device(): call(main_kernel, vmem(7) + [pl.BlockSpec(memory_space=pl.ANY)], (array(N...  1.44 us
    pallas_call x1, Pallas kernels, on_device(): call(pack_y_kernel, smem(1) + vmem(2), (array(Y_ROWS, 128),) * 2)  0.72 us
    pallas_call x1, Pallas kernels, on_device(): call(pack_x_kernel, smem(2) + vmem(2), (array(X_ROWS, 128),) * 2)  0.67 us
    ppermute x6, waiting for transfers between devices, swap(): return lax.ppermute(block, axis, ahead + [(j, i) for i, j in ahead])  0.6 us
  transfers between devices with their start and end apart: 6, of which 2 were waited for; matrix products, arithmetic and copies ran while one was open for 0% of the time, Pallas kernels for 9%

profile of v1, /device:TPU:0, one launch (start us, length us, event | category | flops | bytes accessed | tf_op | source)
XLA Modules:
  0.0 25.9 jit_solution(1244080720469055447)
XLA Ops:
  0.0 0.0 copy-start.1
  0.0 0.9 %copy-done.1 = f32[3,32,4,128]{3,2,1,0:T(4,128)S(1)} copy-done((f32[3,32,4,128]{3,2,1,0:T(4,128)S(1)}, f32[3,32,4,128]{3,2,1,0:T(4,128)}, u32[]{:S(2)}) %copy-start.1) | copy-done | bytes 196632
  0.9 0.0 copy-start.4
  0.9 0.9 %copy-done.4 = f32[1,1,256,128]{3,2,1,0:T(8,128)S(1)} copy-done((f32[1,1,256,128]{3,2,1,0:T(8,128)S(1)}, f32[1,1,256,128]{3,2,1,0:T(8,128)}, u32[]{:S(2)}) %copy-start.4) | copy-done | bytes 131096
  1.8 0.0 copy-start.9
  1.8 0.7 %copy-done.9 = s32[1,1,2,32]{3,2,1,0:T(2,128)S(1)} copy-done((s32[1,1,2,32]{3,2,1,0:T(2,128)S(1)}, s32[1,1,2,32]{3,2,1,0:T(2,128)}, u32[]{:S(2)}) %copy-start.9) | copy-done | bytes 280
  2.5 0.0 copy-start.11
  2.5 0.7 %copy-done.11 = s32[1,1,128]{2,1,0:T(1,128)S(1)} copy-done((s32[1,1,128]{2,1,0:T(1,128)S(1)}, s32[1,1,128]{2,1,0:T(1,128)}, u32[]{:S(2)}) %copy-start.11) | copy-done | bytes 536
  3.2 0.0 copy-start.6
  3.2 0.7 %shard_map.82 = (f32[216,128]{1,0:T(8,128)S(1)}, f32[216,128]{1,0:T(8,128)S(1)}) custom-call(s32[128]{0:T(128)S(1)} %bitcast.20, s32[2,32]{1,0:T(2,128)S(1)} %bitcast.18, f32[256,128]{1,0:T(8,128)S(1)} %bitcast.13, f32[384,128]{1,0:T(8,128)S(1)} %bitcast.10), custom_call_target="tpu_custom_call" | custom-call | flops 1000 | bytes 1000 | tf_op jit(solution)/shard_map/pallas_call | solution.py:402
  3.9 6.0 %collective-permute-start = (f32[216,128]{1,0:T(8,128)S(1)}, f32[216,128]{1,0:T(8,128)S(1)}, u32[]{:S(2)}, u32[]{:S(2)}) collective-permute-start(f32[216,128]{1,0:T(8,128)S(1)} %get-tuple-element.16), channel_id=1, source_target_pairs={{4,8},{12,16},{20,24},{28,0},{8,4},{16,12},{24,20},{0,28},{5,9},{1... | collective-permute-start | bytes 331784 | tf_op jit(solution)/shard_map/ppermute | solution.py:392
  9.9 0.0 collective-permute-start.1
  9.9 0.0 copy-start.2
  9.9 0.9 %copy-done.2 = f32[3,32,4,128]{3,2,1,0:T(4,128)S(1)} copy-done((f32[3,32,4,128]{3,2,1,0:T(4,128)S(1)}, f32[3,32,4,128]{3,2,1,0:T(4,128)}, u32[]{:S(2)}) %copy-start.2) | copy-done | bytes 196632
  10.8 0.0 copy-start.5
  10.8 0.9 %copy-done.5 = f32[1,1,256,128]{3,2,1,0:T(8,128)S(1)} copy-done((f32[1,1,256,128]{3,2,1,0:T(8,128)S(1)}, f32[1,1,256,128]{3,2,1,0:T(8,128)}, u32[]{:S(2)}) %copy-start.5) | copy-done | bytes 131096
  11.7 0.0 copy-start.10
  11.7 0.7 %copy-done.10 = s32[1,1,2,64]{3,2,1,0:T(2,128)S(1)} copy-done((s32[1,1,2,64]{3,2,1,0:T(2,128)S(1)}, s32[1,1,2,64]{3,2,1,0:T(2,128)}, u32[]{:S(2)}) %copy-start.10) | copy-done | bytes 536
  12.4 0.7 %shard_map.83 = (f32[96,128]{1,0:T(8,128)S(1)}, f32[96,128]{1,0:T(8,128)S(1)}) custom-call(s32[2,64]{1,0:T(2,128)S(1)} %bitcast.19, f32[256,128]{1,0:T(8,128)S(1)} %bitcast.14, f32[384,128]{1,0:T(8,128)S(1)} %bitcast.11), custom_call_target="tpu_custom_call" | custom-call | flops 1000 | bytes 1000 | tf_op jit(solution)/shard_map/pallas_call | solution.py:407
  13.1 0.7 %collective-permute-start.2 = (f32[96,128]{1,0:T(8,128)S(1)}, f32[96,128]{1,0:T(8,128)S(1)}, u32[]{:S(2)}, u32[]{:S(2)}) collective-permute-start(f32[96,128]{1,0:T(8,128)S(1)} %get-tuple-element.18), channel_id=1, source_target_pairs={{1,2},{3,0},{2,1},{0,3},{5,6},{7,4},{6,5},{4,7},{9,10},{11,8},{10,... | collective-permute-start | bytes 147464 | tf_op jit(solution)/shard_map/ppermute | solution.py:392
  13.9 1.0 %collective-permute-start.3 = (f32[96,128]{1,0:T(8,128)S(1)}, f32[96,128]{1,0:T(8,128)S(1)}, u32[]{:S(2)}, u32[]{:S(2)}) collective-permute-start(f32[96,128]{1,0:T(8,128)S(1)} %get-tuple-element.19), channel_id=1, source_target_pairs={{0,1},{2,3},{1,0},{3,2},{4,5},{6,7},{5,4},{7,6},{8,9},{10,11},{9,8... | collective-permute-start | bytes 147464 | tf_op jit(solution)/shard_map/ppermute | solution.py:392
  14.8 0.0 collective-permute-done.s0
  14.8 0.5 %collective-permute-done.1.t0 = f32[216,128]{1,0:T(8,128)S(1)} collective-permute-done((f32[216,128]{1,0:T(8,128)S(1)}, f32[216,128]{1,0:T(8,128)S(1)}, u32[]{:S(2)}, u32[]{:S(2)}) %collective-permute-start.1) | collective-permute-done | bytes 110624 | tf_op jit(solution)/shard_map/ppermute | solution.py:392
  15.3 0.1 shard_map.85
  15.4 0.7 %collective-permute-start.4 = (f32[40,128]{1,0:T(8,128)S(1)}, f32[40,128]{1,0:T(8,128)S(1)}, u32[]{:S(2)}, u32[]{:S(2)}) collective-permute-start(f32[40,128]{1,0:T(8,128)S(1)} %get-tuple-element.23), channel_id=1, source_target_pairs={{1,2},{3,0},{2,1},{0,3},{5,6},{7,4},{6,5},{4,7},{9,10},{11,8},{10,... | collective-permute-start | bytes 61448 | tf_op jit(solution)/shard_map/ppermute | solution.py:392
  16.1 1.0 %collective-permute-start.5 = (f32[40,128]{1,0:T(8,128)S(1)}, f32[40,128]{1,0:T(8,128)S(1)}, u32[]{:S(2)}, u32[]{:S(2)}) collective-permute-start(f32[40,128]{1,0:T(8,128)S(1)} %get-tuple-element.24), channel_id=1, source_target_pairs={{0,1},{2,3},{1,0},{3,2},{4,5},{6,7},{5,4},{7,6},{8,9},{10,11},{9,8... | collective-permute-start | bytes 61448 | tf_op jit(solution)/shard_map/ppermute | solution.py:392
  17.1 0.1 collective-permute-done.2.y1
  17.2 0.0 collective-permute-done.3.y0
  17.2 0.0 copy-start
  17.2 2.2 %copy-done = bf16[1,1,256,64,128]{4,3,2,1,0:T(8,128)(2,1)S(1)} copy-done((bf16[1,1,256,64,128]{4,3,2,1,0:T(8,128)(2,1)S(1)}, bf16[1,1,256,64,128]{4,3,2,1,0:T(8,128)(2,1)}, u32[]{:S(2)}) %copy-start) | copy-done | bytes 4194328
  19.4 0.0 copy-start.3
  19.4 0.9 %copy-done.3 = f32[3,32,4,128]{3,2,1,0:T(4,128)S(1)} copy-done((f32[3,32,4,128]{3,2,1,0:T(4,128)S(1)}, f32[3,32,4,128]{3,2,1,0:T(4,128)}, u32[]{:S(2)}) %copy-start.3) | copy-done | bytes 196632
  20.3 0.0 copy-start.7
  20.3 0.7 %copy-done.7 = s32[1,1,2,256]{3,2,1,0:T(2,128)S(1)} copy-done((s32[1,1,2,256]{3,2,1,0:T(2,128)S(1)}, s32[1,1,2,256]{3,2,1,0:T(2,128)}, u32[]{:S(2)}) %copy-start.7) | copy-done | bytes 2072
  21.0 0.0 copy-start.8
  21.0 0.7 %copy-done.8 = s32[1,1,2,256]{3,2,1,0:T(2,128)S(1)} copy-done((s32[1,1,2,256]{3,2,1,0:T(2,128)S(1)}, s32[1,1,2,256]{3,2,1,0:T(2,128)}, u32[]{:S(2)}) %copy-start.8) | copy-done | bytes 2072
  21.6 1.4 %shard_map.84 = (f32[256,128]{1,0:T(8,128)S(1)}, f32[256,128]{1,0:T(8,128)S(1)}, f32[3,48,128]{2,1,0:T(8,128)S(1)}, bf16[512,640]{1,0:T(8,128)(2,1)S(1)}, bf16[16384,128]{1,0:T(8,128)(2,1)S(1)}) custom-call(f32[384,128]{1,0:T(8,128)S(1)} %bitcast.12, f32[216,128]{1,0:T(8,128)S(1)} %collective-permute-done.s0, f32[216,128]{1,0:T(8,128)S(1)} %collective-permute-done.1.t0, ...), custom_call_target="tpu_custom_call" | custom-call | flops 4000000 | bytes 4000000 | tf_op jit(solution)/shard_map/pallas_call | solution.py:415
  23.1 0.0 collective-permute-done.4.ry1
  23.1 0.0 collective-permute-done.5.ry0
  23.1 0.0 copy-done.6
  23.1 2.8 %shard_map.86 = f32[256,128]{1,0:T(8,128)} custom-call(f32[256,128]{1,0:T(8,128)S(1)} %get-tuple-element.20.lm_in, f32[256,128]{1,0:T(8,128)S(1)} %get-tuple-element.21.mm_in, f32[3,48,128]{2,1,0:T(8,128)S(1)} %get-tuple-element.22.strips, f32[40,128]{1,0:T(8,128)S(1)} %collective-permute-done.4.ry1, f32[40,128]{1,0:T(8,128)S(1)} %collective-permute-done.5.ry0, ...), custom_call_target="tpu_custom_call" | custom-call | flops 1000 | bytes 1000 | tf_op jit(solution)/shard_map/pallas_call | solution.py:432
Async XLA Ops:
  0.0 0.9 %copy-start.1 = (f32[3,32,4,128]{3,2,1,0:T(4,128)S(1)}, f32[3,32,4,128]{3,2,1,0:T(4,128)}, u32[]{:S(2)}) copy-start(f32[3,32,4,128]{3,2,1,0:T(4,128)} %param.8) | copy-start | bytes 589828
  0.9 0.9 %copy-start.4 = (f32[1,1,256,128]{3,2,1,0:T(8,128)S(1)}, f32[1,1,256,128]{3,2,1,0:T(8,128)}, u32[]{:S(2)}) copy-start(f32[1,1,256,128]{3,2,1,0:T(8,128)} %param.9) | copy-start | bytes 393220
  1.8 0.7 %copy-start.9 = (s32[1,1,2,32]{3,2,1,0:T(2,128)S(1)}, s32[1,1,2,32]{3,2,1,0:T(2,128)}, u32[]{:S(2)}) copy-start(s32[1,1,2,32]{3,2,1,0:T(2,128)} %param.12) | copy-start | bytes 772
  2.5 0.7 %copy-start.11 = (s32[1,1,128]{2,1,0:T(1,128)S(1)}, s32[1,1,128]{2,1,0:T(1,128)}, u32[]{:S(2)}) copy-start(s32[1,1,128]{2,1,0:T(1,128)} %param.10) | copy-start | bytes 1540
  3.2 19.9 %copy-start.6 = (f32[1,1,256,128]{3,2,1,0:T(8,128)S(1)}, f32[1,1,256,128]{3,2,1,0:T(8,128)}, u32[]{:S(2)}) copy-start(f32[1,1,256,128]{3,2,1,0:T(8,128)} %param.9) | copy-start | bytes 393220
  3.9 11.0 %collective-permute-start = (f32[216,128]{1,0:T(8,128)S(1)}, f32[216,128]{1,0:T(8,128)S(1)}, u32[]{:S(2)}, u32[]{:S(2)}) collective-permute-start(f32[216,128]{1,0:T(8,128)S(1)} %get-tuple-element.16), channel_id=1, source_target_pairs={{4,8},{12,16},{20,24},{28,0},{8,4},{16,12},{24,20},{0,28},{5,9},{1... | collective-permute-start | bytes 331784 | tf_op jit(solution)/shard_map/ppermute | solution.py:392
  9.9 5.4 %collective-permute-start.1 = (f32[216,128]{1,0:T(8,128)S(1)}, f32[216,128]{1,0:T(8,128)S(1)}, u32[]{:S(2)}, u32[]{:S(2)}) collective-permute-start(f32[216,128]{1,0:T(8,128)S(1)} %get-tuple-element.17), channel_id=1, source_target_pairs={{0,4},{8,12},{16,20},{24,28},{4,0},{12,8},{20,16},{28,24},{1,5},{9... | collective-permute-start | bytes 331784 | tf_op jit(solution)/shard_map/ppermute | solution.py:392
  9.9 0.9 %copy-start.2 = (f32[3,32,4,128]{3,2,1,0:T(4,128)S(1)}, f32[3,32,4,128]{3,2,1,0:T(4,128)}, u32[]{:S(2)}) copy-start(f32[3,32,4,128]{3,2,1,0:T(4,128)} %param.8) | copy-start | bytes 589828
  10.8 0.9 %copy-start.5 = (f32[1,1,256,128]{3,2,1,0:T(8,128)S(1)}, f32[1,1,256,128]{3,2,1,0:T(8,128)}, u32[]{:S(2)}) copy-start(f32[1,1,256,128]{3,2,1,0:T(8,128)} %param.9) | copy-start | bytes 393220
  11.7 0.7 %copy-start.10 = (s32[1,1,2,64]{3,2,1,0:T(2,128)S(1)}, s32[1,1,2,64]{3,2,1,0:T(2,128)}, u32[]{:S(2)}) copy-start(s32[1,1,2,64]{3,2,1,0:T(2,128)} %param.11) | copy-start | bytes 1540
  13.1 4.0 %collective-permute-start.2 = (f32[96,128]{1,0:T(8,128)S(1)}, f32[96,128]{1,0:T(8,128)S(1)}, u32[]{:S(2)}, u32[]{:S(2)}) collective-permute-start(f32[96,128]{1,0:T(8,128)S(1)} %get-tuple-element.18), channel_id=1, source_target_pairs={{1,2},{3,0},{2,1},{0,3},{5,6},{7,4},{6,5},{4,7},{9,10},{11,8},{10,... | collective-permute-start | bytes 147464 | tf_op jit(solution)/shard_map/ppermute | solution.py:392
  13.9 3.3 %collective-permute-start.3 = (f32[96,128]{1,0:T(8,128)S(1)}, f32[96,128]{1,0:T(8,128)S(1)}, u32[]{:S(2)}, u32[]{:S(2)}) collective-permute-start(f32[96,128]{1,0:T(8,128)S(1)} %get-tuple-element.19), channel_id=1, source_target_pairs={{0,1},{2,3},{1,0},{3,2},{4,5},{6,7},{5,4},{7,6},{8,9},{10,11},{9,8... | collective-permute-start | bytes 147464 | tf_op jit(solution)/shard_map/ppermute | solution.py:392
  15.4 7.7 %collective-permute-start.4 = (f32[40,128]{1,0:T(8,128)S(1)}, f32[40,128]{1,0:T(8,128)S(1)}, u32[]{:S(2)}, u32[]{:S(2)}) collective-permute-start(f32[40,128]{1,0:T(8,128)S(1)} %get-tuple-element.23), channel_id=1, source_target_pairs={{1,2},{3,0},{2,1},{0,3},{5,6},{7,4},{6,5},{4,7},{9,10},{11,8},{10,... | collective-permute-start | bytes 61448 | tf_op jit(solution)/shard_map/ppermute | solution.py:392
  16.1 7.0 %collective-permute-start.5 = (f32[40,128]{1,0:T(8,128)S(1)}, f32[40,128]{1,0:T(8,128)S(1)}, u32[]{:S(2)}, u32[]{:S(2)}) collective-permute-start(f32[40,128]{1,0:T(8,128)S(1)} %get-tuple-element.24), channel_id=1, source_target_pairs={{0,1},{2,3},{1,0},{3,2},{4,5},{6,7},{5,4},{7,6},{8,9},{10,11},{9,8... | collective-permute-start | bytes 61448 | tf_op jit(solution)/shard_map/ppermute | solution.py:392
  17.2 2.2 %copy-start = (bf16[1,1,256,64,128]{4,3,2,1,0:T(8,128)(2,1)S(1)}, bf16[1,1,256,64,128]{4,3,2,1,0:T(8,128)(2,1)}, u32[]{:S(2)}) copy-start(bf16[1,1,256,64,128]{4,3,2,1,0:T(8,128)(2,1)} %param.15) | copy-start | bytes 12582916
  19.4 0.9 %copy-start.3 = (f32[3,32,4,128]{3,2,1,0:T(4,128)S(1)}, f32[3,32,4,128]{3,2,1,0:T(4,128)}, u32[]{:S(2)}) copy-start(f32[3,32,4,128]{3,2,1,0:T(4,128)} %param.8) | copy-start | bytes 589828
  20.3 0.7 %copy-start.7 = (s32[1,1,2,256]{3,2,1,0:T(2,128)S(1)}, s32[1,1,2,256]{3,2,1,0:T(2,128)}, u32[]{:S(2)}) copy-start(s32[1,1,2,256]{3,2,1,0:T(2,128)} %param.13) | copy-start | bytes 6148
  21.0 0.7 %copy-start.8 = (s32[1,1,2,256]{3,2,1,0:T(2,128)S(1)}, s32[1,1,2,256]{3,2,1,0:T(2,128)}, u32[]{:S(2)}) copy-start(s32[1,1,2,256]{3,2,1,0:T(2,128)} %param.14) | copy-start | bytes 6148

commit v2 on v1

--- a/solution.py
+++ b/solution.py
@@ -20,11 +20,12 @@
 DIAG1_AT = CAPD + 24
 UP_AT = 2 * CAPD + 24
 X_ROWS = UP_AT + CAPX
+BACK_ROWS = 24
 Y_ROWS = CAPY + CX
 R_ROWS = CAPD + 8
 
-POOL = NBD + CAPX + 2 * CAPY + 2 * CAPD
-POOL_PAD = 640
+POOL = NBD + CAPX + 2 * CAPY
+POOL_DIAG = 128
 UP_POOL = NBD
 LOW_POOL = NBD + CAPX
 HIGH_POOL = LOW_POOL + CAPY
@@ -32,6 +33,9 @@
 DIAG_HIGH_POOL = DIAG_LOW_POOL + CAPD
 
 EXT = 48
+GROUP = 8 * 64
+EARLY = 12
+SECOND = 10
 F32 = jnp.float32
 BF16 = jnp.bfloat16
 
@@ -49,36 +53,50 @@
     return lax.rem(lax.axis_index(axis), 2) == 1
 
 
-def pack_x_kernel(up_list, diag_list, rows, vel, s0, t0):
-    is_odd = odd("gx")
-
-    def gather(out):
-        for i in range(CAPD):
-            out[i : i + 1, :] = rows[pl.ds(diag_list[0, i], 1), :]
-            out[DIAG1_AT + i : DIAG1_AT + i + 1, :] = rows[pl.ds(diag_list[1, i], 1), :]
-        for i in range(CAPX):
-            out[UP_AT + i : UP_AT + i + 1, :] = rows[pl.ds(up_list[i], 1), :]
-
-    def edge(out, at):
-        for c in range(3):
-            out[VEL_AT + 8 * c : VEL_AT + 8 * c + 8, :] = vel[c * 128 + at : c * 128 + at + 8, :]
-
-    @pl.when(is_odd)
-    def _():
-        gather(s0)
-        edge(s0, 120)
-        edge(t0, 0)
-
-    @pl.when(jnp.logical_not(is_odd))
-    def _():
-        gather(t0)
-        edge(t0, 120)
-        edge(s0, 0)
-
-
-def pack_y_kernel(side_list, rows, vel, y1, y0):
+def pack_x_kernel(
+    up_hbm, diag_hbm, rows_hbm, vel_hbm, ahead, rows, vel, up_list, diag_list, sems
+):
+    fetches = [
+        pltpu.make_async_copy(source, target, sems.at[n])
+        for n, (source, target) in enumerate(
+            ((up_hbm, up_list), (diag_hbm, diag_list), (rows_hbm, rows), (vel_hbm, vel))
+        )
+    ]
+    for fetch in fetches:
+        fetch.start()
+    for fetch in fetches[:3]:
+        fetch.wait()
+    for i in range(CAPD):
+        ahead[i : i + 1, :] = rows[pl.ds(diag_list[0, i], 1), :]
+        ahead[DIAG1_AT + i : DIAG1_AT + i + 1, :] = rows[pl.ds(diag_list[1, i], 1), :]
+    for i in range(CAPX):
+        ahead[UP_AT + i : UP_AT + i + 1, :] = rows[pl.ds(up_list[i], 1), :]
+    fetches[3].wait()
+    for c in range(3):
+        ahead[VEL_AT + 8 * c : VEL_AT + 8 * c + 8, :] = vel[c * 128 + 120 : c * 128 + 128, :]
+
+
+def weight_copy(weights, start, held, sem):
+    return pltpu.make_async_copy(
+        weights.at[pl.ds(start * GROUP, held.shape[0]), :], held, sem
+    )
+
+
+def pack_y(sources, outs, side_list, sems, weight_copies):
+    side_hbm, tiles_hbm, slots_hbm, rows, vel = sources
+    y1, y0, tiles, slots = outs
     is_odd = odd("gy")
     first = jnp.where(is_odd, 0, 1)
+    fetches = [
+        pltpu.make_async_copy(source, target, sems.at[n])
+        for n, (source, target) in enumerate(
+            ((side_hbm, side_list), (tiles_hbm, tiles), (slots_hbm, slots))
+        )
+    ]
+    fetches += weight_copies
+    for fetch in fetches:
+        fetch.start()
+    fetches[0].wait()
     for i in range(CAPY):
         y1[i : i + 1, :] = rows[pl.ds(side_list[first, i], 1), :]
         y0[i : i + 1, :] = rows[pl.ds(side_list[1 - first, i], 1), :]
@@ -96,27 +114,65 @@
         at = CAPY + 8 * xv
         y1[at : at + 8, :] = jnp.where(is_odd, plus, minus)
         y0[at : at + 8, :] = jnp.where(is_odd, minus, plus)
-
-
-def relay_kernel(s0, t0, ry1, ry0):
-    x_odd = odd("gx")
+    for fetch in fetches[1:]:
+        fetch.wait()
+
+
+def early_kernel(
+    side, tiles_hbm, slots_hbm, weights, rows, vel, back, y1, y0, tiles, slots, held,
+    side_list, sems, sem,
+):
+    for c in range(3):
+        back[8 * c : 8 * c + 8, :] = vel[c * 128 : c * 128 + 8, :]
+
+    @pl.when(lax.axis_index("gx") == 0)
+    def _():
+        sources = (side, tiles_hbm, slots_hbm, rows, vel)
+        copies = [weight_copy(weights, 0, held, sem)]
+        pack_y(sources, (y1, y0, tiles, slots), side_list, sems, copies)
+
+
+def late_kernel(
+    side, tiles_hbm, slots_hbm, weights, rows, vel, _y1, _y0, _tiles, _slots, _held,
+    y1, y0, tiles, slots, held, second, side_list, sems, sem, sem2,
+):
+    @pl.when(lax.axis_index("gx") != 0)
+    def _():
+        sources = (side, tiles_hbm, slots_hbm, rows, vel)
+        copies = [
+            weight_copy(weights, 0, held, sem),
+            weight_copy(weights, EARLY, second, sem2),
+        ]
+        pack_y(sources, (y1, y0, tiles, slots), side_list, sems, copies)
+
+
+def fill_kernel(weights, held, _second, second, turned, sem):
+    copy = weight_copy(weights, EARLY, second, sem)
+
+    @pl.when(lax.axis_index("gx") == 0)
+    def _():
+        copy.start()
+
+    for n in range(2 * EARLY):
+        turned[128 * n : 128 * n + 128, :] = jnp.transpose(held[256 * n : 256 * n + 256, :])
+
+    @pl.when(lax.axis_index("gx") == 0)
+    def _():
+        copy.wait()
+
+
+def relay_kernel(upper, lower, _turned, ry1, ry0):
     y_odd = odd("gy")
-
-    def upper(at):
-        return jnp.where(x_odd, t0[at : at + 8, :], s0[at : at + 8, :])
-
-    def lower(at):
-        return jnp.where(x_odd, s0[at : at + 8, :], t0[at : at + 8, :])
-
     for i in range(0, CAPD, 8):
-        plus, minus = upper(i), upper(DIAG1_AT + i)
+        plus, minus = upper[i : i + 8, :], upper[DIAG1_AT + i : DIAG1_AT + i + 8, :]
         ry1[i : i + 8, :] = jnp.where(y_odd, plus, minus)
         ry0[i : i + 8, :] = jnp.where(y_odd, minus, plus)
     lane = lanes_of((8, 128))
     plus = jnp.zeros((8, 128), F32)
     minus = jnp.zeros((8, 128), F32)
     for c in range(3):
-        for k, part in enumerate((upper(VEL_AT + 8 * c), lower(VEL_AT + 8 * c))):
+        parts = (upper[VEL_AT + 8 * c : VEL_AT + 8 * c + 8, :], lower[8 * c : 8 * c + 8, :])
+        for k, part in enumerate(parts):
             base = (2 * c + k) * 8
             here = (lane >= base) & (lane < base + 2)
             plus = jnp.where(here, roll_lanes(part, base - 126), plus)
@@ -207,21 +263,31 @@
             emit(p, r, lm, mm)
 
 
+def candidates(pool, at, value):
+    high = value.astype(BF16)
+    size = value.shape[0]
+    pool[at : at + size, 0:128] = high
+    pool[at : at + size, 128:256] = (value - high.astype(F32)).astype(BF16)
+
+
 def main_kernel(
-    vel, s0, t0, y1, y0, tiles, slots, weights, lm, mm, strips, picks, held, u, q, sem
+    vel, upper, lower, y1, y0, rows, tiles, slots, weights,
+    lm, mm, strips, partial, diag_picks, third,
+    u, q, picks, pool, picked, sem,
 ):
-    fetch = pltpu.make_async_copy(weights, held, sem)
-    fetch.start()
-    x_odd, y_odd = odd("gx"), odd("gy")
+    fetch = weight_copy(weights, EARLY + SECOND, third, sem)
+
+    @pl.when(lax.axis_index("gx") >= 0)
+    def _():
+        fetch.start()
+
+    y_odd = odd("gy")
     lane = lanes_of((8, 128))
     for c in range(3):
         for z in range(LZ):
-            at = VEL_AT + 8 * c + z
-            s_rows = s0[pl.ds(at, 2, stride=4), :]
-            t_rows = t0[pl.ds(at, 2, stride=4), :]
-            u[c, z, 0:2, :] = jnp.where(x_odd, t_rows, s_rows)
+            u[c, z, 0:2, :] = upper[pl.ds(VEL_AT + 8 * c + z, 2, stride=4), :]
             u[c, z, 2 : CX + 2, :] = vel[pl.ds(c * 128 + z, CX, stride=4), :]
-            u[c, z, CX + 2 : CX + 4, :] = jnp.where(x_odd, s_rows, t_rows)
+            u[c, z, CX + 2 : CX + 4, :] = lower[pl.ds(8 * c + z, 2, stride=4), :]
     for c in range(3):
         for r in range(0, CX + 8, 8):
             strip = jnp.zeros((8, 128), F32)
@@ -257,46 +323,69 @@
         index = index + jnp.where(tile == n, start, 0)
     index = index.astype(F32)
     column = lanes_of((128, 128)).astype(F32)
+    hits = []
     for k in range(2):
         for half in range(2):
             line = index[k : k + 1, half * 128 : half * 128 + 128]
             wanted = jnp.transpose(jnp.broadcast_to(line, (128, 128)))
-            for part in range(POOL_PAD // 128):
-                hit = wanted == column + 128.0 * part
-                at = k * NBD + half * 128
-                picks[at : at + 128, part * 128 : part * 128 + 128] = jnp.where(
-                    hit, 1.0, 0.0
-                ).astype(BF16)
+            at = k * NBD + half * 128
+            for part in range(POOL // 128):
+                hit = jnp.where(wanted == column + 128.0 * part, 1.0, 0.0)
+                picks[at : at + 128, part * 128 : part * 128 + 128] = hit.astype(BF16)
+            hit = (wanted - (POOL - 64.0 * k)) == column
+            mine = (column >= 64.0) if k else (column < 64.0)
+            hits.append(jnp.where(hit & mine, 1.0, 0.0))
+    for half in range(2):
+        diag_picks[half * 128 : half * 128 + 128, :] = (hits[half] + hits[2 + half]).astype(BF16)
+    candidates(pool, 0, rows[...])
+    candidates(pool, UP_POOL, upper[UP_AT:, :])
+    candidates(pool, LOW_POOL, jnp.where(y_odd, y0[:CAPY, :], y1[:CAPY, :]))
+    candidates(pool, HIGH_POOL, jnp.where(y_odd, y1[:CAPY, :], y0[:CAPY, :]))
+    picked[...] = jnp.dot(picks[...], pool[...], preferred_element_type=F32)
+    front = lane < 64
+    for r in range(0, NBD, 8):
+        for n in range(2):
+            first = picked[r : r + 8, 128 * n : 128 * n + 128]
+            second = picked[NBD + r : NBD + r + 8, 128 * n : 128 * n + 128]
+            partial[r : r + 8, 128 * n : 128 * n + 128] = jnp.where(
+                front, first, roll_lanes(second, 64)
+            )
+            partial[r : r + 8, 256 + 128 * n : 384 + 128 * n] = jnp.where(
+                front, roll_lanes(first, 64), second
+            )
     fetch.wait()
 
 
 def final_kernel(
-    lm_in, mm_in, strips, ry1, ry0, s0, t0, y1, y0, rows, picks, weights, out,
-    u, q, lm, mm, pool, picked,
+    lm_in, mm_in, strips, ry1, ry0, partial, picks, turned, second, third, out,
+    u, q, lm, mm, pool, picked, lefts, departs,
 ):
-    x_odd, y_odd = odd("gx"), odd("gy")
+    y_odd = odd("gy")
     lane = lanes_of((8, 128))
     lm[...] = lm_in[...]
     mm[...] = mm_in[...]
 
-    def candidates(at, value):
-        high = value.astype(BF16)
-        size = value.shape[0]
-        pool[at : at + size, 0:128] = high
-        pool[at : at + size, 128:256] = (value - high.astype(F32)).astype(BF16)
-
-    candidates(0, rows[...])
-    candidates(UP_POOL, jnp.where(x_odd, t0[UP_AT:, :], s0[UP_AT:, :]))
-    candidates(LOW_POOL, jnp.where(y_odd, y0[:CAPY, :], y1[:CAPY, :]))
-    candidates(HIGH_POOL, jnp.where(y_odd, y1[:CAPY, :], y0[:CAPY, :]))
-    candidates(DIAG_LOW_POOL, jnp.where(y_odd, ry0[:CAPD, :], ry1[:CAPD, :]))
-    candidates(DIAG_HIGH_POOL, jnp.where(y_odd, ry1[:CAPD, :], ry0[:CAPD, :]))
-    pool[POOL:, :] = jnp.zeros((POOL_PAD - POOL, 256), BF16)
-    picked[...] = jnp.dot(picks[...], pool[...], preferred_element_type=F32)
+    diag = jnp.concatenate(
+        [
+            jnp.where(y_odd, ry0[:CAPD, :], ry1[:CAPD, :]),
+            jnp.where(y_odd, ry1[:CAPD, :], ry0[:CAPD, :]),
+        ],
+        axis=0,
+    )
+    high = diag.astype(BF16).astype(F32)
+    front = lanes_of((2 * CAPD, 128)) < 64
+    for n, term in enumerate((high, diag - high)):
+        swapped = roll_lanes(term, 64)
+        for at, value in (
+            (128 * n, (jnp.where(front, term, 0.0), jnp.where(front, 0.0, swapped))),
+            (256 + 128 * n, (jnp.where(front, swapped, 0.0), jnp.where(front, 0.0, term))),
+        ):
+            pool[: 2 * CAPD, at : at + 128] = value[0].astype(BF16)
+            pool[2 * CAPD :, at : at + 128] = value[1].astype(BF16)
+    picked[...] = partial[...] + jnp.dot(picks[...], pool[...], preferred_element_type=F32)
 
     low = jnp.where(y_odd, ry0[CAPD:, :], ry1[CAPD:, :])
     high = jnp.where(y_odd, ry1[CAPD:, :], ry0[CAPD:, :])
-    level = lane // 32
     u[...] = strips[...].reshape(u.shape)
     for c in range(3):
         for k, at in enumerate((0, CX + 2)):
@@ -312,7 +401,6 @@
                     here = (one >= 32 * z + 20) & (one < 32 * z + 22)
                     row = jnp.where(here, roll_lanes(line, 32 * z + 20 - base), row)
                 u[c, 0, at + x : at + x + 1, :] = row
-    del level
 
     def emit(_, r, lm_part, mm_part):
         for into, part in ((lm, lm_part), (mm, mm_part)):
@@ -327,31 +415,46 @@
     stencil(u, q, 1, strip_diff, emit)
 
     row_of = lax.broadcasted_iota(jnp.int32, (8, 128), 0)
+    top = lax.broadcasted_iota(jnp.int32, (16, 128), 0) % 8 < 4
+    for x in range(CX):
+        for n in range(2):
+            left = jnp.concatenate(
+                [
+                    picked[8 * x : 8 * x + 8, 128 * n + at : 128 * n + at + 128]
+                    for at in (0, 256)
+                ],
+                axis=0,
+            )
+            at = 32 * x + 16 * n
+            lefts[at : at + 16, :128] = jnp.where(top, left, 0.0).astype(BF16)
+            lefts[at : at + 16, 128:] = jnp.where(top, 0.0, left).astype(BF16)
+    for x in range(CX):
+        if x < EARLY:
+            right, over = turned[256 * x : 256 * x + 256, :], 0
+        else:
+            late = x >= EARLY + SECOND
+            held, at = (third, x - EARLY - SECOND) if late else (second, x - EARLY)
+            at = GROUP * at
+            right = jnp.concatenate([held[at : at + 256, :], held[at + 256 : at + 512, :]], axis=1)
+            over = 1
+        product = lax.dot_general(
+            lefts[32 * x : 32 * x + 32, :],
+            right,
+            (((1,), (over,)), ((), ())),
+            preferred_element_type=F32,
+        )
+        product = product[:16] + product[16:]
+        for n in range(2):
+            part = product[8 * n : 8 * n + 8, :]
+            departs[n, 8 * x : 8 * x + 8, :] = jnp.where(
+                row_of % 4 < 2, part[:, :128], part[:, 128:]
+            )
+
     front = lane < 64
     even = row_of % 2 == 0
     for x in range(CX):
-        terms = []
-        for half in range(2):
-            first = picked[8 * x : 8 * x + 8, 128 * half : 128 * half + 128]
-            second = picked[NBD + 8 * x : NBD + 8 * x + 8, 128 * half : 128 * half + 128]
-            terms.append(jnp.where(front, first, roll_lanes(second, 64)))
-            terms.append(jnp.where(front, roll_lanes(first, 64), second))
-        left = jnp.concatenate(terms, axis=0).astype(BF16)
-        product = lax.dot_general(
-            left,
-            weights[512 * x : 512 * x + 512, :],
-            (((1,), (1,)), ((), ())),
-            preferred_element_type=F32,
-        )
-        product = product[:16] + product[16:]
-        found = []
-        for at in (0, 8):
-            merged = product[at : at + 8, 384:512]
-            for part in (2, 1, 0):
-                mine = row_of // 2 == part
-                merged = jnp.where(mine, product[at : at + 8, 128 * part : 128 * part + 128], merged)
-            found.append(merged)
-        lm_depart, mm_depart = found
+        lm_depart = departs[0, 8 * x : 8 * x + 8, :]
+        mm_depart = departs[1, 8 * x : 8 * x + 8, :]
         lm_block, mm_block = lm[8 * x : 8 * x + 8, :], mm[8 * x : 8 * x + 8, :]
         ratio = (TIME_STEP / 1.5) * jnp.exp(0.125 * jnp.log(lm_depart * mm_depart))
         weight = ratio / (1.0 + ratio)
@@ -366,23 +469,24 @@
     return [pl.BlockSpec(memory_space=pltpu.VMEM)] * count
 
 
-def smem(count=1):
-    return [pl.BlockSpec(memory_space=pltpu.SMEM)] * count
+def hbm(count=1):
+    return [pl.BlockSpec(memory_space=pltpu.HBM)] * count
 
 
 def array(*shape, dtype=F32):
     return jax.ShapeDtypeStruct(shape, dtype)
 
 
-def call(kernel, ins, outs, scratch=(), flops=1000):
+def call(kernel, ins, outs, scratch=(), cost=1000, aliases=()):
     return pl.pallas_call(
         kernel,
         in_specs=ins,
         out_specs=tuple(vmem(len(outs))) if isinstance(outs, tuple) else vmem()[0],
         out_shape=outs,
         scratch_shapes=list(scratch),
+        input_output_aliases=dict(aliases),
         compiler_params=pltpu.CompilerParams(vmem_limit_bytes=32 * 1024 * 1024),
-        cost_estimate=pl.CostEstimate(flops=flops, bytes_accessed=flops, transcendentals=0),
+        cost_estimate=pl.CostEstimate(flops=cost, bytes_accessed=cost, transcendentals=0),
     )
 
 
@@ -392,56 +496,108 @@
     return lax.ppermute(block, axis, ahead + [(j, i) for i, j in ahead])
 
 
+def shift(block, axis, distance):
+    count = lax.axis_size(axis)
+    return lax.ppermute(block, axis, [(i, (i + distance) % count) for i in range(count)])
+
+
 def on_device(
     velocity, pair_blocks, send_up, send_side, send_diag, depart_tile, depart_slot, interp_weights
 ):
-    vel = velocity.reshape(3 * CX * LZ, 128)
-    rows = pair_blocks[0, 0]
-    weights = interp_weights.reshape(NBD * 64, 128)
-
-    s0, t0 = call(pack_x_kernel, smem(2) + vmem(2), (array(X_ROWS, 128),) * 2)(
-        send_up[0, 0], send_diag[0, 0], rows, vel
+    def stay(x):
+        return pltpu.with_memory_space_constraint(x, pltpu.HBM)
+
+    vel = stay(velocity.reshape(3 * CX * LZ, 128))
+    rows = stay(pair_blocks[0, 0])
+    weights = stay(interp_weights.reshape(NBD * 64, 128))
+    up, side, diag = stay(send_up[0, 0]), stay(send_side[0, 0]), stay(send_diag[0, 0])
+    tiles, slots = stay(depart_tile[0, 0]), stay(depart_slot[0, 0])
+
+    ahead, held_rows, held_vel = call(
+        pack_x_kernel,
+        hbm(4),
+        (array(X_ROWS, 128), array(*rows.shape), array(*vel.shape)),
+        [
+            pltpu.SMEM((CAPX,), jnp.int32),
+            pltpu.SMEM((2, CAPD), jnp.int32),
+            pltpu.SemaphoreType.DMA((4,)),
+        ],
+    )(up, diag, rows, vel)
+    upper = shift(ahead, "gx", 1)
+    def held(count):
+        return array(count * GROUP, 128, dtype=BF16)
+
+    packed = (
+        array(Y_ROWS, 128),
+        array(Y_ROWS, 128),
+        array(*tiles.shape, dtype=jnp.int32),
+        array(*slots.shape, dtype=jnp.int32),
+        held(EARLY),
     )
-    s0 = swap(s0, "gx", 1)
-    t0 = swap(t0, "gx", 0)
-    y1, y0 = call(pack_y_kernel, smem(1) + vmem(2), (array(Y_ROWS, 128),) * 2)(
-        send_side[0, 0], rows, vel
-    )
+    scratch = [pltpu.SMEM((2, CAPY), jnp.int32), pltpu.SemaphoreType.DMA((3,))]
+    sources = (side, tiles, slots, weights, held_rows, held_vel)
+    back, *early = call(
+        early_kernel,
+        hbm(4) + vmem(2),
+        (array(BACK_ROWS, 128),) + packed,
+        scratch + [pltpu.SemaphoreType.DMA],
+    )(*sources)
+    lower = shift(back, "gx", -1)
+    y1, y0, held_tiles, held_slots, first, second = call(
+        late_kernel,
+        hbm(4) + vmem(7),
+        packed + (held(SECOND),),
+        scratch + [pltpu.SemaphoreType.DMA] * 2,
+        aliases=((6 + n, n) for n in range(5)),
+    )(*sources, *early)
     y1 = swap(y1, "gy", 1)
     y0 = swap(y0, "gy", 0)
-    ry1, ry0 = call(relay_kernel, vmem(2), (array(R_ROWS, 128),) * 2)(s0, t0)
+    second, turned = call(
+        fill_kernel,
+        hbm() + vmem(2),
+        (held(SECOND), array(EARLY * 256, 256, dtype=BF16)),
+        [pltpu.SemaphoreType.DMA],
+        aliases=((2, 0),),
+    )(weights, first, second)
+    ry1, ry0 = call(relay_kernel, vmem(3), (array(R_ROWS, 128),) * 2, cost=300000000)(upper, lower, turned)
     ry1 = swap(ry1, "gy", 1)
     ry0 = swap(ry0, "gy", 0)
-    lm, mm, strips, picks, held = call(
+    lm, mm, strips, partial, picks, third = call(
         main_kernel,
-        vmem(7) + [pl.BlockSpec(memory_space=pl.ANY)],
+        vmem(8) + hbm(),
         (
             array(NBD, 128),
             array(NBD, 128),
             array(3, EXT, 128),
-            array(2 * NBD, POOL_PAD, dtype=BF16),
-            array(NBD * 64, 128, dtype=BF16),
+            array(NBD, 512),
+            array(NBD, POOL_DIAG, dtype=BF16),
+            held(NBD // 8 - EARLY - SECOND),
         ),
         [
             pltpu.VMEM((3, LZ, EXT, 128), F32),
             pltpu.VMEM((15, LZ, EXT, 128), F32),
+            pltpu.VMEM((2 * NBD, POOL), BF16),
+            pltpu.VMEM((POOL, 256), BF16),
+            pltpu.VMEM((2 * NBD, 256), F32),
             pltpu.SemaphoreType.DMA,
         ],
-        flops=4000000,
-    )(vel, s0, t0, y1, y0, depart_tile[0, 0], depart_slot[0, 0], weights)
+        cost=5000000,
+    )(held_vel, upper, lower, y1, y0, held_rows, held_tiles, held_slots, weights)
     result = call(
         final_kernel,
-        vmem(12),
+        vmem(10),
         array(NBD, 128),
         [
             pltpu.VMEM((3, 1, EXT, 128), F32),
             pltpu.VMEM((15, 1, EXT, 128), F32),
             pltpu.VMEM((NBD, 128), F32),
             pltpu.VMEM((NBD, 128), F32),
-            pltpu.VMEM((POOL_PAD, 256), BF16),
-            pltpu.VMEM((2 * NBD, 256), F32),
+            pltpu.VMEM((POOL_DIAG, 512), BF16),
+            pltpu.VMEM((NBD, 512), F32),
+            pltpu.VMEM((4 * NBD, 256), BF16),
+            pltpu.VMEM((2, NBD, 128), F32),
         ],
-    )(lm, mm, strips, ry1, ry0, s0, t0, y1, y0, rows, picks, held)
+    )(lm, mm, strips, ry1, ry0, partial, picks, turned, second, third)
     return result[None, None]
 
 

time: 26.3 us -> 16.3 us (0.62)
  local copies, waits for them, and re-layouts: 10.2 us -> 0 us
  Pallas kernels: 5.74 us -> 7.78 us
  starting transfers between devices: 9.4 us -> 8.11 us
  waiting for transfers between devices: 0.6 us -> 0.1 us
    unnamed x24 -> x0, local copies, waits for them, and re-layouts: 10.2 us -> none
    ppermute x6 -> x4, starting transfers between devices: 9.4 us -> 3.44 us  [swap(): return lax.ppermute(block, axis, ahead + [(j, i) for i, j in ahead])]
    ppermute x0 -> x2, starting transfers between devices: none -> 4.67 us  [shift(): lax.ppermute(block, axis, [(i, (i + distance) % count) for i in range(cou...]
    pallas_call x5 -> x7, Pallas kernels: 5.74 us -> 7.78 us  [the longest x1 2.17 us: on_device(): call(final_kernel, vmem(10), array(NBD, 128), [pltpu.VMEM((3, 1, EXT, 128...]
    ppermute x6 -> x4, waiting for transfers between devices: 0.6 us -> 0.1 us  [swap(): return lax.ppermute(block, axis, ahead + [(j, i) for i, j in ahead])]
  transfers between devices with their start and end apart: 6 -> 6, of which waited for: 2 -> 1; matrix products, arithmetic and copies ran while one was open for 0% -> 0% of each run, Pallas kernels for 9% -> 28%
where the time goes in v2:
time: 16.3 us; the launch traced here: 16.1 us
  starting transfers between devices  8.11 us (50%)
  Pallas kernels  7.78 us (48%)
    ppermute x2, starting transfers between devices, shift(): lax.ppermute(block, axis, [(i, (i + distance) % count) for i in range(cou...  4.67 us
    ppermute x4, starting transfers between devices, swap(): return lax.ppermute(block, axis, ahead + [(j, i) for i, j in ahead])  3.44 us
    pallas_call x1, Pallas kernels, on_device(): call(final_kernel, vmem(10), array(NBD, 128), [pltpu.VMEM((3, 1, EXT, 128...  2.17 us
    pallas_call x1, Pallas kernels, on_device(): call(main_kernel, vmem(8) + hbm(), (array(NBD, 128), array(NBD, 128), arr...  1.62 us
    pallas_call x1, Pallas kernels, on_device(): call(early_kernel, hbm(4) + vmem(2), (array(BACK_ROWS, 128),) + packed, s...  1.48 us
    pallas_call x1, Pallas kernels, on_device(): call(fill_kernel, hbm() + vmem(2), (held(SECOND), array(EARLY * 256, 256,...  1.33 us
    pallas_call x1, Pallas kernels, on_device(): call(pack_x_kernel, hbm(4), (array(X_ROWS, 128), array(*rows.shape), arra...  1.04 us
  transfers between devices with their start and end apart: 6, of which 1 were waited for; matrix products, arithmetic and copies ran while one was open for 0% of the time, Pallas kernels for 28%

profile of v2, /device:TPU:0, one launch (start us, length us, event | category | flops | bytes accessed | tf_op | source)
XLA Modules:
  0.0 16.1 jit_solution(10754663659523351621)
XLA Ops:
  0.0 1.0 %shard_map.82 = (f32[216,128]{1,0:T(8,128)S(1)}, f32[256,128]{1,0:T(8,128)S(1)}, f32[384,128]{1,0:T(8,128)S(1)}) custom-call(s32[128]{0:T(128)} %bitcast.22, s32[2,32]{1,0:T(2,128)} %bitcast.21, f32[256,128]{1,0:T(8,128)} %bitcast.14, f32[384,128]{1,0:T(8,128)} %bitcast.13), custom_call_target="tpu_custom_call" | custom-call | flops 1000 | bytes 1000 | tf_op jit(solution)/shard_map/pallas_call | solution.py:516
  1.1 3.0 %collective-permute-start = (f32[216,128]{1,0:T(8,128)S(1)}, f32[216,128]{1,0:T(8,128)S(1)}, u32[]{:S(2)}, u32[]{:S(2)}) collective-permute-start(f32[216,128]{1,0:T(8,128)S(1)} %get-tuple-element.31), channel_id=1, source_target_pairs={{0,4},{4,8},{8,12},{12,16},{16,20},{20,24},{24,28},{28,0},{1,5},{5... | collective-permute-start | bytes 331784 | tf_op jit(solution)/shard_map/ppermute | solution.py:501
  4.0 1.5 %shard_map.83 = (f32[24,128]{1,0:T(8,128)S(1)}, f32[96,128]{1,0:T(8,128)S(1)}, f32[96,128]{1,0:T(8,128)S(1)}, s32[2,256]{1,0:T(2,128)S(1)}, s32[2,256]{1,0:T(2,128)S(1)}, /*index=5*/bf16[6144,128]{1,0:T(8,128)(2,1)S(1)}) custom-call(s32[2,64]{1,0:T(2,128)} %bitcast.19, s32[2,256]{1,0:T(2,128)} %bitcast.15, s32[2,256]{1,0:T(2,128)} %bitcast.17, ...), custom_call_target="tpu_custom_call" | custom-call | flops 1000 | bytes 1000 | tf_op jit(solution)/shard_map/pallas_call | solution.py:539
  5.5 1.7 %collective-permute-start.1 = (f32[24,128]{1,0:T(8,128)S(1)}, f32[24,128]{1,0:T(8,128)S(1)}, u32[]{:S(2)}, u32[]{:S(2)}) collective-permute-start(f32[24,128]{1,0:T(8,128)S(1)} %get-tuple-element.33), channel_id=1, source_target_pairs={{0,28},{4,0},{8,4},{12,8},{16,12},{20,16},{24,20},{28,24},{1,29},{... | collective-permute-start | bytes 36872 | tf_op jit(solution)/shard_map/ppermute | solution.py:501
  7.3 0.7 %collective-permute-start.2 = (f32[96,128]{1,0:T(8,128)S(1)}, f32[96,128]{1,0:T(8,128)S(1)}, u32[]{:S(2)}, u32[]{:S(2)}) collective-permute-start(f32[96,128]{1,0:T(8,128)S(1)} %get-tuple-element.39), channel_id=1, source_target_pairs={{1,2},{3,0},{2,1},{0,3},{5,6},{7,4},{6,5},{4,7},{9,10},{11,8},{10,... | collective-permute-start | bytes 147464 | tf_op jit(solution)/shard_map/ppermute | solution.py:496
  8.0 1.1 %collective-permute-start.3 = (f32[96,128]{1,0:T(8,128)S(1)}, f32[96,128]{1,0:T(8,128)S(1)}, u32[]{:S(2)}, u32[]{:S(2)}) collective-permute-start(f32[96,128]{1,0:T(8,128)S(1)} %get-tuple-element.40), channel_id=1, source_target_pairs={{0,1},{2,3},{1,0},{3,2},{4,5},{6,7},{5,4},{7,6},{8,9},{10,11},{9,8... | collective-permute-start | bytes 147464 | tf_op jit(solution)/shard_map/ppermute | solution.py:496
  9.1 1.3 %shard_map.86 = (bf16[5120,128]{1,0:T(8,128)(2,1)S(1)}, bf16[3072,256]{1,0:T(8,128)(2,1)S(1)}) custom-call(bf16[16384,128]{1,0:T(8,128)(2,1)} %bitcast.11, bf16[6144,128]{1,0:T(8,128)(2,1)S(1)} %get-tuple-element.46.held, bf16[5120,128]{1,0:T(8,128)(2,1)S(1)} %get-tuple-element.47._second), custom_call_target="tpu_custom_call", output_to_operand_aliasing={{0}: (2, {})} | custom-call | flops 1000 | bytes 1000 | tf_op jit(solution)/shard_map/pallas_call | solution.py:555
  10.5 0.0 collective-permute-done.1.lower
  10.5 0.0 collective-permute-done.upper
  10.5 0.1 shard_map.87
  10.6 0.1 collective-permute-start.4
  10.7 1.4 %collective-permute-start.5 = (f32[40,128]{1,0:T(8,128)S(1)}, f32[40,128]{1,0:T(8,128)S(1)}, u32[]{:S(2)}, u32[]{:S(2)}) collective-permute-start(f32[40,128]{1,0:T(8,128)S(1)} %get-tuple-element.50), channel_id=1, source_target_pairs={{0,1},{2,3},{1,0},{3,2},{4,5},{6,7},{5,4},{7,6},{8,9},{10,11},{9,8... | collective-permute-start | bytes 61448 | tf_op jit(solution)/shard_map/ppermute | solution.py:496
  12.2 0.0 collective-permute-done.2.y1
  12.2 0.0 collective-permute-done.3.y0
  12.2 1.6 %shard_map.85 = (f32[256,128]{1,0:T(8,128)S(1)}, f32[256,128]{1,0:T(8,128)S(1)}, f32[3,48,128]{2,1,0:T(8,128)S(1)}, f32[256,512]{1,0:T(8,128)S(1)}, bf16[256,128...) custom-call(f32[384,128]{1,0:T(8,128)S(1)} %get-tuple-element.30.vel, f32[216,128]{1,0:T(8,128)S(1)} %collective-permute-done.upper, ...), custom_call_target="tpu_custom_call" | custom-call | flops 5000000 | bytes 5000000 | tf_op jit(solution)/shard_map/pallas_call | solution.py:565
  13.8 0.1 collective-permute-done.4.ry1
  13.9 0.0 collective-permute-done.5.ry0
  13.9 2.2 %shard_map.88 = f32[256,128]{1,0:T(8,128)} custom-call(f32[256,128]{1,0:T(8,128)S(1)} %get-tuple-element.43.lm_in, f32[256,128]{1,0:T(8,128)S(1)} %get-tuple-element.44.mm_in, f32[3,48,128]{2,1,0:T(8,128)S(1)} %get-tuple-element.45.strips, f32[40,128]{1,0:T(8,128)S(1)} %collective-permute-done.4.ry1, f32[40,128]{1,0:T(8,128)S(1)} %collective-permute-done.5.ry0, ...), custom_call_target="tpu_custom_call" | custom-call | flops 1000 | bytes 1000 | tf_op jit(solution)/shard_map/pallas_call | solution.py:586
  (1 shorter events, 0.0 us)
Async XLA Ops:
  1.1 9.4 %collective-permute-start = (f32[216,128]{1,0:T(8,128)S(1)}, f32[216,128]{1,0:T(8,128)S(1)}, u32[]{:S(2)}, u32[]{:S(2)}) collective-permute-start(f32[216,128]{1,0:T(8,128)S(1)} %get-tuple-element.31), channel_id=1, source_target_pairs={{0,4},{4,8},{8,12},{12,16},{16,20},{20,24},{24,28},{28,0},{1,5},{5... | collective-permute-start | bytes 331784 | tf_op jit(solution)/shard_map/ppermute | solution.py:501
  5.5 4.9 %collective-permute-start.1 = (f32[24,128]{1,0:T(8,128)S(1)}, f32[24,128]{1,0:T(8,128)S(1)}, u32[]{:S(2)}, u32[]{:S(2)}) collective-permute-start(f32[24,128]{1,0:T(8,128)S(1)} %get-tuple-element.33), channel_id=1, source_target_pairs={{0,28},{4,0},{8,4},{12,8},{16,12},{20,16},{24,20},{28,24},{1,29},{... | collective-permute-start | bytes 36872 | tf_op jit(solution)/shard_map/ppermute | solution.py:501
  7.3 4.9 %collective-permute-start.2 = (f32[96,128]{1,0:T(8,128)S(1)}, f32[96,128]{1,0:T(8,128)S(1)}, u32[]{:S(2)}, u32[]{:S(2)}) collective-permute-start(f32[96,128]{1,0:T(8,128)S(1)} %get-tuple-element.39), channel_id=1, source_target_pairs={{1,2},{3,0},{2,1},{0,3},{5,6},{7,4},{6,5},{4,7},{9,10},{11,8},{10,... | collective-permute-start | bytes 147464 | tf_op jit(solution)/shard_map/ppermute | solution.py:496
  8.0 4.1 %collective-permute-start.3 = (f32[96,128]{1,0:T(8,128)S(1)}, f32[96,128]{1,0:T(8,128)S(1)}, u32[]{:S(2)}, u32[]{:S(2)}) collective-permute-start(f32[96,128]{1,0:T(8,128)S(1)} %get-tuple-element.40), channel_id=1, source_target_pairs={{0,1},{2,3},{1,0},{3,2},{4,5},{6,7},{5,4},{7,6},{8,9},{10,11},{9,8... | collective-permute-start | bytes 147464 | tf_op jit(solution)/shard_map/ppermute | solution.py:496
  10.6 3.3 %collective-permute-start.4 = (f32[40,128]{1,0:T(8,128)S(1)}, f32[40,128]{1,0:T(8,128)S(1)}, u32[]{:S(2)}, u32[]{:S(2)}) collective-permute-start(f32[40,128]{1,0:T(8,128)S(1)} %get-tuple-element.49), channel_id=1, source_target_pairs={{1,2},{3,0},{2,1},{0,3},{5,6},{7,4},{6,5},{4,7},{9,10},{11,8},{10,... | collective-permute-start | bytes 61448 | tf_op jit(solution)/shard_map/ppermute | solution.py:496
  10.7 3.2 %collective-permute-start.5 = (f32[40,128]{1,0:T(8,128)S(1)}, f32[40,128]{1,0:T(8,128)S(1)}, u32[]{:S(2)}, u32[]{:S(2)}) collective-permute-start(f32[40,128]{1,0:T(8,128)S(1)} %get-tuple-element.50), channel_id=1, source_target_pairs={{0,1},{2,3},{1,0},{3,2},{4,5},{6,7},{5,4},{7,6},{8,9},{10,11},{9,8... | collective-permute-start | bytes 61448 | tf_op jit(solution)/shard_map/ppermute | solution.py:496

commit v3 on v2

--- a/solution.py
+++ b/solution.py
@@ -35,7 +35,7 @@
 EXT = 48
 GROUP = 8 * 64
 EARLY = 12
-SECOND = 10
+SECOND = 6
 F32 = jnp.float32
 BF16 = jnp.bfloat16
 
@@ -77,9 +77,7 @@
 
 
 def weight_copy(weights, start, held, sem):
-    return pltpu.make_async_copy(
-        weights.at[pl.ds(start * GROUP, held.shape[0]), :], held, sem
-    )
+    return pltpu.make_async_copy(weights.at[pl.ds(start * GROUP, held.shape[0]), :], held, sem)
 
 
 def pack_y(sources, outs, side_list, sems, weight_copies):
@@ -133,9 +131,16 @@
 
 
 def late_kernel(
-    side, tiles_hbm, slots_hbm, weights, rows, vel, _y1, _y0, _tiles, _slots, _held,
+    side, tiles_hbm, slots_hbm, weights, rows, vel, y1_early, y0_early, tiles_early, slots_early,
     y1, y0, tiles, slots, held, second, side_list, sems, sem, sem2,
 ):
+    @pl.when(lax.axis_index("gx") == 0)
+    def _():
+        y1[...] = y1_early[...]
+        y0[...] = y0_early[...]
+        tiles[...] = tiles_early[...]
+        slots[...] = slots_early[...]
+
     @pl.when(lax.axis_index("gx") != 0)
     def _():
         sources = (side, tiles_hbm, slots_hbm, rows, vel)
@@ -146,19 +151,28 @@
         pack_y(sources, (y1, y0, tiles, slots), side_list, sems, copies)
 
 
-def fill_kernel(weights, held, _second, second, turned, sem):
+def turn(held, turned):
+    for n in range(2 * EARLY):
+        turned[128 * n : 128 * n + 128, :] = jnp.transpose(held[256 * n : 256 * n + 256, :])
+
+
+def fill_kernel(weights, held_early, held_late, second_late, second, turned, sem):
     copy = weight_copy(weights, EARLY, second, sem)
 
     @pl.when(lax.axis_index("gx") == 0)
     def _():
         copy.start()
 
-    for n in range(2 * EARLY):
-        turned[128 * n : 128 * n + 128, :] = jnp.transpose(held[256 * n : 256 * n + 256, :])
-
-    @pl.when(lax.axis_index("gx") == 0)
+        @after_start
+        def _():
+            turn(held_early, turned)
+
+        copy.wait()
+
+    @pl.when(lax.axis_index("gx") != 0)
     def _():
-        copy.wait()
+        second[...] = second_late[...]
+        turn(held_late, turned)
 
 
 def relay_kernel(upper, lower, _turned, ry1, ry0):
@@ -263,6 +277,10 @@
             emit(p, r, lm, mm)
 
 
+def after_start(body):
+    pl.loop(0, jnp.where(lax.axis_index("gx") >= 0, 1, 0))(lambda _: body())
+
+
 def candidates(pool, at, value):
     high = value.astype(BF16)
     size = value.shape[0]
@@ -277,82 +295,83 @@
 ):
     fetch = weight_copy(weights, EARLY + SECOND, third, sem)
 
-    @pl.when(lax.axis_index("gx") >= 0)
+    fetch.start()
+
+    @after_start
     def _():
-        fetch.start()
-
-    y_odd = odd("gy")
-    lane = lanes_of((8, 128))
-    for c in range(3):
-        for z in range(LZ):
-            u[c, z, 0:2, :] = upper[pl.ds(VEL_AT + 8 * c + z, 2, stride=4), :]
-            u[c, z, 2 : CX + 2, :] = vel[pl.ds(c * 128 + z, CX, stride=4), :]
-            u[c, z, CX + 2 : CX + 4, :] = lower[pl.ds(8 * c + z, 2, stride=4), :]
-    for c in range(3):
-        for r in range(0, CX + 8, 8):
-            strip = jnp.zeros((8, 128), F32)
+        y_odd = odd("gy")
+        lane = lanes_of((8, 128))
+        for c in range(3):
             for z in range(LZ):
-                base = 32 * z
-                plane = u[c, z, r : r + 8, :]
-                left = (lane >= base + 2) & (lane < base + 6)
-                right = (lane >= base + 16) & (lane < base + 20)
-                strip = jnp.where(left, roll_lanes(plane, base + 2), strip)
-                strip = jnp.where(right, roll_lanes(plane, base + 16 - 124), strip)
-            strips[c, r : r + 8, :] = strip
-        for r in range(0, CX, 8):
-            at = CAPY + r
-            low = jnp.where(y_odd, y0[at : at + 8, :], y1[at : at + 8, :])
-            high = jnp.where(y_odd, y1[at : at + 8, :], y0[at : at + 8, :])
-            strip = strips[c, r + 2 : r + 10, :]
-            strip = jnp.where(lane % 32 < 2, roll_lanes(low, -8 * c), strip)
-            here = (lane % 32 >= 20) & (lane % 32 < 22)
-            strip = jnp.where(here, roll_lanes(high, 20 - 8 * c), strip)
-            strips[c, r + 2 : r + 10, :] = strip
-
-    def emit(z, r, lm_part, mm_part):
+                u[c, z, 0:2, :] = upper[pl.ds(VEL_AT + 8 * c + z, 2, stride=4), :]
+                u[c, z, 2 : CX + 2, :] = vel[pl.ds(c * 128 + z, CX, stride=4), :]
+                u[c, z, CX + 2 : CX + 4, :] = lower[pl.ds(8 * c + z, 2, stride=4), :]
+        for c in range(3):
+            for r in range(0, CX + 8, 8):
+                strip = jnp.zeros((8, 128), F32)
+                for z in range(LZ):
+                    base = 32 * z
+                    plane = u[c, z, r : r + 8, :]
+                    left = (lane >= base + 2) & (lane < base + 6)
+                    right = (lane >= base + 16) & (lane < base + 20)
+                    strip = jnp.where(left, roll_lanes(plane, base + 2), strip)
+                    strip = jnp.where(right, roll_lanes(plane, base + 16 - 124), strip)
+                strips[c, r : r + 8, :] = strip
+            for r in range(0, CX, 8):
+                at = CAPY + r
+                low = jnp.where(y_odd, y0[at : at + 8, :], y1[at : at + 8, :])
+                high = jnp.where(y_odd, y1[at : at + 8, :], y0[at : at + 8, :])
+                strip = strips[c, r + 2 : r + 10, :]
+                strip = jnp.where(lane % 32 < 2, roll_lanes(low, -8 * c), strip)
+                here = (lane % 32 >= 20) & (lane % 32 < 22)
+                strip = jnp.where(here, roll_lanes(high, 20 - 8 * c), strip)
+                strips[c, r + 2 : r + 10, :] = strip
+
+        def emit(z, r, lm_part, mm_part):
+            for k in range(2):
+                lm[pl.ds(8 * r + 2 * z + k, 8, stride=8), :] = lm_part
+                mm[pl.ds(8 * r + 2 * z + k, 8, stride=8), :] = mm_part
+
+        stencil(u, q, LZ, plane_diff, emit)
+
+        tile = tiles[...]
+        starts = (0, UP_POOL, LOW_POOL, HIGH_POOL, DIAG_LOW_POOL, DIAG_HIGH_POOL)
+        index = slots[...]
+        for n, start in enumerate(starts):
+            index = index + jnp.where(tile == n, start, 0)
+        index = index.astype(F32)
+        column = lanes_of((128, 128)).astype(F32)
+        hits = []
         for k in range(2):
-            lm[pl.ds(8 * r + 2 * z + k, 8, stride=8), :] = lm_part
-            mm[pl.ds(8 * r + 2 * z + k, 8, stride=8), :] = mm_part
-
-    stencil(u, q, LZ, plane_diff, emit)
-
-    tile = tiles[...]
-    starts = (0, UP_POOL, LOW_POOL, HIGH_POOL, DIAG_LOW_POOL, DIAG_HIGH_POOL)
-    index = slots[...]
-    for n, start in enumerate(starts):
-        index = index + jnp.where(tile == n, start, 0)
-    index = index.astype(F32)
-    column = lanes_of((128, 128)).astype(F32)
-    hits = []
-    for k in range(2):
+            for half in range(2):
+                line = index[k : k + 1, half * 128 : half * 128 + 128]
+                wanted = jnp.transpose(jnp.broadcast_to(line, (128, 128)))
+                at = k * NBD + half * 128
+                for part in range(POOL // 128):
+                    hit = jnp.where(wanted == column + 128.0 * part, 1.0, 0.0)
+                    picks[at : at + 128, part * 128 : part * 128 + 128] = hit.astype(BF16)
+                hit = (wanted - (POOL - 64.0 * k)) == column
+                mine = (column >= 64.0) if k else (column < 64.0)
+                hits.append(jnp.where(hit & mine, 1.0, 0.0))
         for half in range(2):
-            line = index[k : k + 1, half * 128 : half * 128 + 128]
-            wanted = jnp.transpose(jnp.broadcast_to(line, (128, 128)))
-            at = k * NBD + half * 128
-            for part in range(POOL // 128):
-                hit = jnp.where(wanted == column + 128.0 * part, 1.0, 0.0)
-                picks[at : at + 128, part * 128 : part * 128 + 128] = hit.astype(BF16)
-            hit = (wanted - (POOL - 64.0 * k)) == column
-            mine = (column >= 64.0) if k else (column < 64.0)
-            hits.append(jnp.where(hit & mine, 1.0, 0.0))
-    for half in range(2):
-        diag_picks[half * 128 : half * 128 + 128, :] = (hits[half] + hits[2 + half]).astype(BF16)
-    candidates(pool, 0, rows[...])
-    candidates(pool, UP_POOL, upper[UP_AT:, :])
-    candidates(pool, LOW_POOL, jnp.where(y_odd, y0[:CAPY, :], y1[:CAPY, :]))
-    candidates(pool, HIGH_POOL, jnp.where(y_odd, y1[:CAPY, :], y0[:CAPY, :]))
-    picked[...] = jnp.dot(picks[...], pool[...], preferred_element_type=F32)
-    front = lane < 64
-    for r in range(0, NBD, 8):
-        for n in range(2):
-            first = picked[r : r + 8, 128 * n : 128 * n + 128]
-            second = picked[NBD + r : NBD + r + 8, 128 * n : 128 * n + 128]
-            partial[r : r + 8, 128 * n : 128 * n + 128] = jnp.where(
-                front, first, roll_lanes(second, 64)
-            )
-            partial[r : r + 8, 256 + 128 * n : 384 + 128 * n] = jnp.where(
-                front, roll_lanes(first, 64), second
-            )
+            diag_picks[half * 128 : half * 128 + 128, :] = (hits[half] + hits[2 + half]).astype(BF16)
+        candidates(pool, 0, rows[...])
+        candidates(pool, UP_POOL, upper[UP_AT:, :])
+        candidates(pool, LOW_POOL, jnp.where(y_odd, y0[:CAPY, :], y1[:CAPY, :]))
+        candidates(pool, HIGH_POOL, jnp.where(y_odd, y1[:CAPY, :], y0[:CAPY, :]))
+        picked[...] = jnp.dot(picks[...], pool[...], preferred_element_type=F32)
+        front = lane < 64
+        for r in range(0, NBD, 8):
+            for n in range(2):
+                first = picked[r : r + 8, 128 * n : 128 * n + 128]
+                second = picked[NBD + r : NBD + r + 8, 128 * n : 128 * n + 128]
+                partial[r : r + 8, 128 * n : 128 * n + 128] = jnp.where(
+                    front, first, roll_lanes(second, 64)
+                )
+                partial[r : r + 8, 256 + 128 * n : 384 + 128 * n] = jnp.where(
+                    front, roll_lanes(first, 64), second
+                )
+
     fetch.wait()
 
 
@@ -477,14 +496,13 @@
     return jax.ShapeDtypeStruct(shape, dtype)
 
 
-def call(kernel, ins, outs, scratch=(), cost=1000, aliases=()):
+def call(kernel, ins, outs, scratch=(), cost=1000):
     return pl.pallas_call(
         kernel,
         in_specs=ins,
         out_specs=tuple(vmem(len(outs))) if isinstance(outs, tuple) else vmem()[0],
         out_shape=outs,
         scratch_shapes=list(scratch),
-        input_output_aliases=dict(aliases),
         compiler_params=pltpu.CompilerParams(vmem_limit_bytes=32 * 1024 * 1024),
         cost_estimate=pl.CostEstimate(flops=cost, bytes_accessed=cost, transcendentals=0),
     )
@@ -524,6 +542,7 @@
         ],
     )(up, diag, rows, vel)
     upper = shift(ahead, "gx", 1)
+
     def held(count):
         return array(count * GROUP, 128, dtype=BF16)
 
@@ -543,23 +562,23 @@
         scratch + [pltpu.SemaphoreType.DMA],
     )(*sources)
     lower = shift(back, "gx", -1)
-    y1, y0, held_tiles, held_slots, first, second = call(
+    y1, y0, held_tiles, held_slots, late, second = call(
         late_kernel,
-        hbm(4) + vmem(7),
+        hbm(4) + vmem(6),
         packed + (held(SECOND),),
         scratch + [pltpu.SemaphoreType.DMA] * 2,
-        aliases=((6 + n, n) for n in range(5)),
-    )(*sources, *early)
+    )(*sources, *early[:4])
     y1 = swap(y1, "gy", 1)
     y0 = swap(y0, "gy", 0)
     second, turned = call(
         fill_kernel,
-        hbm() + vmem(2),
+        hbm() + vmem(3),
         (held(SECOND), array(EARLY * 256, 256, dtype=BF16)),
         [pltpu.SemaphoreType.DMA],
-        aliases=((2, 0),),
-    )(weights, first, second)
-    ry1, ry0 = call(relay_kernel, vmem(3), (array(R_ROWS, 128),) * 2, cost=300000000)(upper, lower, turned)
+    )(weights, early[4], late, second)
+    ry1, ry0 = call(relay_kernel, vmem(3), (array(R_ROWS, 128),) * 2, cost=300000000)(
+        upper, lower, turned
+    )
     ry1 = swap(ry1, "gy", 1)
     ry0 = swap(ry0, "gy", 0)
     lm, mm, strips, partial, picks, third = call(

time: 16.3 us -> 16.2 us (level)
  Pallas kernels: 7.78 us -> 7.47 us
    pallas_call x2, Pallas kernels: 1.38 us -> 1.19 us  [the longest x1 1.14 us: on_device(): call(fill_kernel, hbm() + vmem(3), (held(SECOND), array(EARLY * 256, 256,...]
  transfers between devices with their start and end apart: 6 -> 6, of which waited for: 1 -> 2; matrix products, arithmetic and copies ran while one was open for 0% -> 0% of each run, Pallas kernels for 28% -> 27%
where the time goes in v3:
time: 16.2 us; the launch traced here: 16 us
  starting transfers between devices  8.24 us (51%)
  Pallas kernels  7.47 us (46%)
  waiting for transfers between devices  0.23 us (1%)
    ppermute x2, starting transfers between devices, shift(): lax.ppermute(block, axis, [(i, (i + distance) % count) for i in range(cou...  4.67 us
    ppermute x4, starting transfers between devices, swap(): return lax.ppermute(block, axis, ahead + [(j, i) for i, j in ahead])  3.56 us
    pallas_call x1, Pallas kernels, on_device(): call(final_kernel, vmem(10), array(NBD, 128), [pltpu.VMEM((3, 1, EXT, 128...  2.17 us
    pallas_call x1, Pallas kernels, on_device(): call(main_kernel, vmem(8) + hbm(), (array(NBD, 128), array(NBD, 128), arr...  1.51 us
    pallas_call x1, Pallas kernels, on_device(): call(early_kernel, hbm(4) + vmem(2), (array(BACK_ROWS, 128),) + packed, s...  1.48 us
    pallas_call x1, Pallas kernels, on_device(): call(fill_kernel, hbm() + vmem(3), (held(SECOND), array(EARLY * 256, 256,...  1.14 us
    pallas_call x1, Pallas kernels, on_device(): call(pack_x_kernel, hbm(4), (array(X_ROWS, 128), array(*rows.shape), arra...  1.04 us
  transfers between devices with their start and end apart: 6, of which 2 were waited for; matrix products, arithmetic and copies ran while one was open for 0% of the time, Pallas kernels for 27%

profile of v3, /device:TPU:0, one launch (start us, length us, event | category | flops | bytes accessed | tf_op | source)
XLA Modules:
  0.0 16.0 jit_solution(9112073142409821055)
XLA Ops:
  0.0 1.0 %shard_map.82 = (f32[216,128]{1,0:T(8,128)S(1)}, f32[256,128]{1,0:T(8,128)S(1)}, f32[384,128]{1,0:T(8,128)S(1)}) custom-call(s32[128]{0:T(128)} %bitcast.22, s32[2,32]{1,0:T(2,128)} %bitcast.21, f32[256,128]{1,0:T(8,128)} %bitcast.14, f32[384,128]{1,0:T(8,128)} %bitcast.13), custom_call_target="tpu_custom_call" | custom-call | flops 1000 | bytes 1000 | tf_op jit(solution)/shard_map/pallas_call | solution.py:534
  1.1 3.0 %collective-permute-start = (f32[216,128]{1,0:T(8,128)S(1)}, f32[216,128]{1,0:T(8,128)S(1)}, u32[]{:S(2)}, u32[]{:S(2)}) collective-permute-start(f32[216,128]{1,0:T(8,128)S(1)} %get-tuple-element.31), channel_id=1, source_target_pairs={{0,4},{4,8},{8,12},{12,16},{16,20},{20,24},{24,28},{28,0},{1,5},{5... | collective-permute-start | bytes 331784 | tf_op jit(solution)/shard_map/ppermute | solution.py:519
  4.0 1.5 %shard_map.83 = (f32[24,128]{1,0:T(8,128)S(1)}, f32[96,128]{1,0:T(8,128)S(1)}, f32[96,128]{1,0:T(8,128)S(1)}, s32[2,256]{1,0:T(2,128)S(1)}, s32[2,256]{1,0:T(2,128)S(1)}, /*index=5*/bf16[6144,128]{1,0:T(8,128)(2,1)S(1)}) custom-call(s32[2,64]{1,0:T(2,128)} %bitcast.19, s32[2,256]{1,0:T(2,128)} %bitcast.15, s32[2,256]{1,0:T(2,128)} %bitcast.17, ...), custom_call_target="tpu_custom_call" | custom-call | flops 1000 | bytes 1000 | tf_op jit(solution)/shard_map/pallas_call | solution.py:558
  5.5 1.7 %collective-permute-start.1 = (f32[24,128]{1,0:T(8,128)S(1)}, f32[24,128]{1,0:T(8,128)S(1)}, u32[]{:S(2)}, u32[]{:S(2)}) collective-permute-start(f32[24,128]{1,0:T(8,128)S(1)} %get-tuple-element.33), channel_id=1, source_target_pairs={{0,28},{4,0},{8,4},{12,8},{16,12},{20,16},{24,20},{28,24},{1,29},{... | collective-permute-start | bytes 36872 | tf_op jit(solution)/shard_map/ppermute | solution.py:519
  7.2 0.1 shard_map.84
  7.3 0.7 %collective-permute-start.2 = (f32[96,128]{1,0:T(8,128)S(1)}, f32[96,128]{1,0:T(8,128)S(1)}, u32[]{:S(2)}, u32[]{:S(2)}) collective-permute-start(f32[96,128]{1,0:T(8,128)S(1)} %get-tuple-element.38), channel_id=1, source_target_pairs={{1,2},{3,0},{2,1},{0,3},{5,6},{7,4},{6,5},{4,7},{9,10},{11,8},{10,... | collective-permute-start | bytes 147464 | tf_op jit(solution)/shard_map/ppermute | solution.py:514
  8.0 1.1 %collective-permute-start.3 = (f32[96,128]{1,0:T(8,128)S(1)}, f32[96,128]{1,0:T(8,128)S(1)}, u32[]{:S(2)}, u32[]{:S(2)}) collective-permute-start(f32[96,128]{1,0:T(8,128)S(1)} %get-tuple-element.39), channel_id=1, source_target_pairs={{0,1},{2,3},{1,0},{3,2},{4,5},{6,7},{5,4},{7,6},{8,9},{10,11},{9,8... | collective-permute-start | bytes 147464 | tf_op jit(solution)/shard_map/ppermute | solution.py:514
  9.1 1.1 %shard_map.86 = (bf16[3072,128]{1,0:T(8,128)(2,1)S(1)}, bf16[3072,256]{1,0:T(8,128)(2,1)S(1)}) custom-call(bf16[16384,128]{1,0:T(8,128)(2,1)} %bitcast.11, bf16[6144,128]{1,0:T(8,128)(2,1)S(1)} %get-tuple-element.45.held_early, bf16[6144,128]{1,0:T(8,128)(2,1)S(1)} %get-tuple-element.46.held_late, bf16[3072,128]{1,0:T(8,128)(2,1)S(1)} %get-tuple-element.47.second_late), custom_call_target="tpu_custom_call" | custom-call | flops 1000 | bytes 1000 | tf_op jit(solution)/shard_map/pallas_call | solution.py:573
  10.3 0.1 collective-permute-done.1.lower
  10.4 0.0 collective-permute-done.upper
  10.4 0.1 shard_map.87
  10.5 0.1 collective-permute-start.4
  10.5 1.6 %collective-permute-start.5 = (f32[40,128]{1,0:T(8,128)S(1)}, f32[40,128]{1,0:T(8,128)S(1)}, u32[]{:S(2)}, u32[]{:S(2)}) collective-permute-start(f32[40,128]{1,0:T(8,128)S(1)} %get-tuple-element.50), channel_id=1, source_target_pairs={{0,1},{2,3},{1,0},{3,2},{4,5},{6,7},{5,4},{7,6},{8,9},{10,11},{9,8... | collective-permute-start | bytes 61448 | tf_op jit(solution)/shard_map/ppermute | solution.py:514
  12.2 0.0 collective-permute-done.2.y1
  12.2 0.0 collective-permute-done.3.y0
  12.2 1.5 %shard_map.85 = (f32[256,128]{1,0:T(8,128)S(1)}, f32[256,128]{1,0:T(8,128)S(1)}, f32[3,48,128]{2,1,0:T(8,128)S(1)}, f32[256,512]{1,0:T(8,128)S(1)}, bf16[256,128...) custom-call(f32[384,128]{1,0:T(8,128)S(1)} %get-tuple-element.30.vel, f32[216,128]{1,0:T(8,128)S(1)} %collective-permute-done.upper, ...), custom_call_target="tpu_custom_call" | custom-call | flops 5000000 | bytes 5000000 | tf_op jit(solution)/shard_map/pallas_call | solution.py:584
  13.7 0.1 collective-permute-done.4.ry1
  13.8 0.0 collective-permute-done.5.ry0
  13.8 2.2 %shard_map.88 = f32[256,128]{1,0:T(8,128)} custom-call(f32[256,128]{1,0:T(8,128)S(1)} %get-tuple-element.42.lm_in, f32[256,128]{1,0:T(8,128)S(1)} %get-tuple-element.43.mm_in, f32[3,48,128]{2,1,0:T(8,128)S(1)} %get-tuple-element.44.strips, f32[40,128]{1,0:T(8,128)S(1)} %collective-permute-done.4.ry1, f32[40,128]{1,0:T(8,128)S(1)} %collective-permute-done.5.ry0, ...), custom_call_target="tpu_custom_call" | custom-call | flops 1000 | bytes 1000 | tf_op jit(solution)/shard_map/pallas_call | solution.py:605
Async XLA Ops:
  1.1 9.3 %collective-permute-start = (f32[216,128]{1,0:T(8,128)S(1)}, f32[216,128]{1,0:T(8,128)S(1)}, u32[]{:S(2)}, u32[]{:S(2)}) collective-permute-start(f32[216,128]{1,0:T(8,128)S(1)} %get-tuple-element.31), channel_id=1, source_target_pairs={{0,4},{4,8},{8,12},{12,16},{16,20},{20,24},{24,28},{28,0},{1,5},{5... | collective-permute-start | bytes 331784 | tf_op jit(solution)/shard_map/ppermute | solution.py:519
  5.5 4.8 %collective-permute-start.1 = (f32[24,128]{1,0:T(8,128)S(1)}, f32[24,128]{1,0:T(8,128)S(1)}, u32[]{:S(2)}, u32[]{:S(2)}) collective-permute-start(f32[24,128]{1,0:T(8,128)S(1)} %get-tuple-element.33), channel_id=1, source_target_pairs={{0,28},{4,0},{8,4},{12,8},{16,12},{20,16},{24,20},{28,24},{1,29},{... | collective-permute-start | bytes 36872 | tf_op jit(solution)/shard_map/ppermute | solution.py:519
  7.3 4.9 %collective-permute-start.2 = (f32[96,128]{1,0:T(8,128)S(1)}, f32[96,128]{1,0:T(8,128)S(1)}, u32[]{:S(2)}, u32[]{:S(2)}) collective-permute-start(f32[96,128]{1,0:T(8,128)S(1)} %get-tuple-element.38), channel_id=1, source_target_pairs={{1,2},{3,0},{2,1},{0,3},{5,6},{7,4},{6,5},{4,7},{9,10},{11,8},{10,... | collective-permute-start | bytes 147464 | tf_op jit(solution)/shard_map/ppermute | solution.py:514
  8.0 4.1 %collective-permute-start.3 = (f32[96,128]{1,0:T(8,128)S(1)}, f32[96,128]{1,0:T(8,128)S(1)}, u32[]{:S(2)}, u32[]{:S(2)}) collective-permute-start(f32[96,128]{1,0:T(8,128)S(1)} %get-tuple-element.39), channel_id=1, source_target_pairs={{0,1},{2,3},{1,0},{3,2},{4,5},{6,7},{5,4},{7,6},{8,9},{10,11},{9,8... | collective-permute-start | bytes 147464 | tf_op jit(solution)/shard_map/ppermute | solution.py:514
  10.5 3.4 %collective-permute-start.4 = (f32[40,128]{1,0:T(8,128)S(1)}, f32[40,128]{1,0:T(8,128)S(1)}, u32[]{:S(2)}, u32[]{:S(2)}) collective-permute-start(f32[40,128]{1,0:T(8,128)S(1)} %get-tuple-element.49), channel_id=1, source_target_pairs={{1,2},{3,0},{2,1},{0,3},{5,6},{7,4},{6,5},{4,7},{9,10},{11,8},{10,... | collective-permute-start | bytes 61448 | tf_op jit(solution)/shard_map/ppermute | solution.py:514
  10.5 3.3 %collective-permute-start.5 = (f32[40,128]{1,0:T(8,128)S(1)}, f32[40,128]{1,0:T(8,128)S(1)}, u32[]{:S(2)}, u32[]{:S(2)}) collective-permute-start(f32[40,128]{1,0:T(8,128)S(1)} %get-tuple-element.50), channel_id=1, source_target_pairs={{0,1},{2,3},{1,0},{3,2},{4,5},{6,7},{5,4},{7,6},{8,9},{10,11},{9,8... | collective-permute-start | bytes 61448 | tf_op jit(solution)/shard_map/ppermute | solution.py:514

commit v4 on v3

--- a/solution.py
+++ b/solution.py
@@ -34,7 +34,7 @@
 
 EXT = 48
 GROUP = 8 * 64
-EARLY = 12
+EARLY = 10
 SECOND = 6
 F32 = jnp.float32
 BF16 = jnp.bfloat16

time: 16.2 us -> 16.1 us (level)
  waiting for transfers between devices: 0.23 us -> 0.03 us
  transfers between devices with their start and end apart: 6 -> 6, of which waited for: 2 -> 0; matrix products, arithmetic and copies ran while one was open for 0% -> 0% of each run, Pallas kernels for 27% -> 27%
where the time goes in v4:
time: 16.1 us; the launch traced here: 15.9 us
  starting transfers between devices  8.3 us (52%)
  Pallas kernels  7.5 us (47%)
    ppermute x2, starting transfers between devices, shift(): lax.ppermute(block, axis, [(i, (i + distance) % count) for i in range(cou...  4.77 us
    ppermute x4, starting transfers between devices, swap(): return lax.ppermute(block, axis, ahead + [(j, i) for i, j in ahead])  3.53 us
    pallas_call x1, Pallas kernels, on_device(): call(final_kernel, vmem(10), array(NBD, 128), [pltpu.VMEM((3, 1, EXT, 128...  2.2 us
    pallas_call x1, Pallas kernels, on_device(): call(main_kernel, vmem(8) + hbm(), (array(NBD, 128), array(NBD, 128), arr...  1.6 us
    pallas_call x1, Pallas kernels, on_device(): call(early_kernel, hbm(4) + vmem(2), (array(BACK_ROWS, 128),) + packed, s...  1.38 us
    pallas_call x1, Pallas kernels, on_device(): call(fill_kernel, hbm() + vmem(3), (held(SECOND), array(EARLY * 256, 256,...  1.14 us
    pallas_call x1, Pallas kernels, on_device(): call(pack_x_kernel, hbm(4), (array(X_ROWS, 128), array(*rows.shape), arra...  1.04 us
  transfers between devices with their start and end apart: 6, of which 0 were waited for; matrix products, arithmetic and copies ran while one was open for 0% of the time, Pallas kernels for 27%

profile of v4, /device:TPU:0, one launch (start us, length us, event | category | flops | bytes accessed | tf_op | source)
XLA Modules:
  0.0 15.9 jit_solution(5343564635435507190)
XLA Ops:
  0.0 1.0 %shard_map.82 = (f32[216,128]{1,0:T(8,128)S(1)}, f32[256,128]{1,0:T(8,128)S(1)}, f32[384,128]{1,0:T(8,128)S(1)}) custom-call(s32[128]{0:T(128)} %bitcast.22, s32[2,32]{1,0:T(2,128)} %bitcast.21, f32[256,128]{1,0:T(8,128)} %bitcast.14, f32[384,128]{1,0:T(8,128)} %bitcast.13), custom_call_target="tpu_custom_call" | custom-call | flops 1000 | bytes 1000 | tf_op jit(solution)/shard_map/pallas_call | solution.py:534
  1.1 3.0 %collective-permute-start = (f32[216,128]{1,0:T(8,128)S(1)}, f32[216,128]{1,0:T(8,128)S(1)}, u32[]{:S(2)}, u32[]{:S(2)}) collective-permute-start(f32[216,128]{1,0:T(8,128)S(1)} %get-tuple-element.31), channel_id=1, source_target_pairs={{0,4},{4,8},{8,12},{12,16},{16,20},{20,24},{24,28},{28,0},{1,5},{5... | collective-permute-start | bytes 331784 | tf_op jit(solution)/shard_map/ppermute | solution.py:519
  4.0 1.4 %shard_map.83 = (f32[24,128]{1,0:T(8,128)S(1)}, f32[96,128]{1,0:T(8,128)S(1)}, f32[96,128]{1,0:T(8,128)S(1)}, s32[2,256]{1,0:T(2,128)S(1)}, s32[2,256]{1,0:T(2,128)S(1)}, /*index=5*/bf16[5120,128]{1,0:T(8,128)(2,1)S(1)}) custom-call(s32[2,64]{1,0:T(2,128)} %bitcast.19, s32[2,256]{1,0:T(2,128)} %bitcast.15, s32[2,256]{1,0:T(2,128)} %bitcast.17, ...), custom_call_target="tpu_custom_call" | custom-call | flops 1000 | bytes 1000 | tf_op jit(solution)/shard_map/pallas_call | solution.py:558
  5.4 1.8 %collective-permute-start.1 = (f32[24,128]{1,0:T(8,128)S(1)}, f32[24,128]{1,0:T(8,128)S(1)}, u32[]{:S(2)}, u32[]{:S(2)}) collective-permute-start(f32[24,128]{1,0:T(8,128)S(1)} %get-tuple-element.33), channel_id=1, source_target_pairs={{0,28},{4,0},{8,4},{12,8},{16,12},{20,16},{24,20},{28,24},{1,29},{... | collective-permute-start | bytes 36872 | tf_op jit(solution)/shard_map/ppermute | solution.py:519
  7.2 0.1 shard_map.84
  7.3 0.7 %collective-permute-start.2 = (f32[96,128]{1,0:T(8,128)S(1)}, f32[96,128]{1,0:T(8,128)S(1)}, u32[]{:S(2)}, u32[]{:S(2)}) collective-permute-start(f32[96,128]{1,0:T(8,128)S(1)} %get-tuple-element.38), channel_id=1, source_target_pairs={{1,2},{3,0},{2,1},{0,3},{5,6},{7,4},{6,5},{4,7},{9,10},{11,8},{10,... | collective-permute-start | bytes 147464 | tf_op jit(solution)/shard_map/ppermute | solution.py:514
  8.0 1.1 %collective-permute-start.3 = (f32[96,128]{1,0:T(8,128)S(1)}, f32[96,128]{1,0:T(8,128)S(1)}, u32[]{:S(2)}, u32[]{:S(2)}) collective-permute-start(f32[96,128]{1,0:T(8,128)S(1)} %get-tuple-element.39), channel_id=1, source_target_pairs={{0,1},{2,3},{1,0},{3,2},{4,5},{6,7},{5,4},{7,6},{8,9},{10,11},{9,8... | collective-permute-start | bytes 147464 | tf_op jit(solution)/shard_map/ppermute | solution.py:514
  9.1 1.1 %shard_map.86 = (bf16[3072,128]{1,0:T(8,128)(2,1)S(1)}, bf16[2560,256]{1,0:T(8,128)(2,1)S(1)}) custom-call(bf16[16384,128]{1,0:T(8,128)(2,1)} %bitcast.11, bf16[5120,128]{1,0:T(8,128)(2,1)S(1)} %get-tuple-element.45.held_early, bf16[5120,128]{1,0:T(8,128)(2,1)S(1)} %get-tuple-element.46.held_late, bf16[3072,128]{1,0:T(8,128)(2,1)S(1)} %get-tuple-element.47.second_late), custom_call_target="tpu_custom_call" | custom-call | flops 1000 | bytes 1000 | tf_op jit(solution)/shard_map/pallas_call | solution.py:573
  10.3 0.0 collective-permute-done.1.lower
  10.3 0.0 collective-permute-done.upper
  10.3 0.1 shard_map.87
  10.4 0.1 collective-permute-start.4
  10.5 1.5 %collective-permute-start.5 = (f32[40,128]{1,0:T(8,128)S(1)}, f32[40,128]{1,0:T(8,128)S(1)}, u32[]{:S(2)}, u32[]{:S(2)}) collective-permute-start(f32[40,128]{1,0:T(8,128)S(1)} %get-tuple-element.50), channel_id=1, source_target_pairs={{0,1},{2,3},{1,0},{3,2},{4,5},{6,7},{5,4},{7,6},{8,9},{10,11},{9,8... | collective-permute-start | bytes 61448 | tf_op jit(solution)/shard_map/ppermute | solution.py:514
  12.1 0.0 collective-permute-done.2.y1
  12.1 0.0 collective-permute-done.3.y0
  12.1 1.6 %shard_map.85 = (f32[256,128]{1,0:T(8,128)S(1)}, f32[256,128]{1,0:T(8,128)S(1)}, f32[3,48,128]{2,1,0:T(8,128)S(1)}, f32[256,512]{1,0:T(8,128)S(1)}, bf16[256,128...) custom-call(f32[384,128]{1,0:T(8,128)S(1)} %get-tuple-element.30.vel, f32[216,128]{1,0:T(8,128)S(1)} %collective-permute-done.upper, ...), custom_call_target="tpu_custom_call" | custom-call | flops 5000000 | bytes 5000000 | tf_op jit(solution)/shard_map/pallas_call | solution.py:584
  13.7 0.0 collective-permute-done.4.ry1
  13.7 0.0 collective-permute-done.5.ry0
  13.7 2.2 %shard_map.88 = f32[256,128]{1,0:T(8,128)} custom-call(f32[256,128]{1,0:T(8,128)S(1)} %get-tuple-element.42.lm_in, f32[256,128]{1,0:T(8,128)S(1)} %get-tuple-element.43.mm_in, f32[3,48,128]{2,1,0:T(8,128)S(1)} %get-tuple-element.44.strips, f32[40,128]{1,0:T(8,128)S(1)} %collective-permute-done.4.ry1, f32[40,128]{1,0:T(8,128)S(1)} %collective-permute-done.5.ry0, ...), custom_call_target="tpu_custom_call" | custom-call | flops 1000 | bytes 1000 | tf_op jit(solution)/shard_map/pallas_call | solution.py:605
Async XLA Ops:
  1.1 9.2 %collective-permute-start = (f32[216,128]{1,0:T(8,128)S(1)}, f32[216,128]{1,0:T(8,128)S(1)}, u32[]{:S(2)}, u32[]{:S(2)}) collective-permute-start(f32[216,128]{1,0:T(8,128)S(1)} %get-tuple-element.31), channel_id=1, source_target_pairs={{0,4},{4,8},{8,12},{12,16},{16,20},{20,24},{24,28},{28,0},{1,5},{5... | collective-permute-start | bytes 331784 | tf_op jit(solution)/shard_map/ppermute | solution.py:519
  5.4 4.9 %collective-permute-start.1 = (f32[24,128]{1,0:T(8,128)S(1)}, f32[24,128]{1,0:T(8,128)S(1)}, u32[]{:S(2)}, u32[]{:S(2)}) collective-permute-start(f32[24,128]{1,0:T(8,128)S(1)} %get-tuple-element.33), channel_id=1, source_target_pairs={{0,28},{4,0},{8,4},{12,8},{16,12},{20,16},{24,20},{28,24},{1,29},{... | collective-permute-start | bytes 36872 | tf_op jit(solution)/shard_map/ppermute | solution.py:519
  7.3 4.8 %collective-permute-start.2 = (f32[96,128]{1,0:T(8,128)S(1)}, f32[96,128]{1,0:T(8,128)S(1)}, u32[]{:S(2)}, u32[]{:S(2)}) collective-permute-start(f32[96,128]{1,0:T(8,128)S(1)} %get-tuple-element.38), channel_id=1, source_target_pairs={{1,2},{3,0},{2,1},{0,3},{5,6},{7,4},{6,5},{4,7},{9,10},{11,8},{10,... | collective-permute-start | bytes 147464 | tf_op jit(solution)/shard_map/ppermute | solution.py:514
  8.0 4.0 %collective-permute-start.3 = (f32[96,128]{1,0:T(8,128)S(1)}, f32[96,128]{1,0:T(8,128)S(1)}, u32[]{:S(2)}, u32[]{:S(2)}) collective-permute-start(f32[96,128]{1,0:T(8,128)S(1)} %get-tuple-element.39), channel_id=1, source_target_pairs={{0,1},{2,3},{1,0},{3,2},{4,5},{6,7},{5,4},{7,6},{8,9},{10,11},{9,8... | collective-permute-start | bytes 147464 | tf_op jit(solution)/shard_map/ppermute | solution.py:514
  10.4 3.3 %collective-permute-start.4 = (f32[40,128]{1,0:T(8,128)S(1)}, f32[40,128]{1,0:T(8,128)S(1)}, u32[]{:S(2)}, u32[]{:S(2)}) collective-permute-start(f32[40,128]{1,0:T(8,128)S(1)} %get-tuple-element.49), channel_id=1, source_target_pairs={{1,2},{3,0},{2,1},{0,3},{5,6},{7,4},{6,5},{4,7},{9,10},{11,8},{10,... | collective-permute-start | bytes 61448 | tf_op jit(solution)/shard_map/ppermute | solution.py:514
  10.5 3.2 %collective-permute-start.5 = (f32[40,128]{1,0:T(8,128)S(1)}, f32[40,128]{1,0:T(8,128)S(1)}, u32[]{:S(2)}, u32[]{:S(2)}) collective-permute-start(f32[40,128]{1,0:T(8,128)S(1)} %get-tuple-element.50), channel_id=1, source_target_pairs={{0,1},{2,3},{1,0},{3,2},{4,5},{6,7},{5,4},{7,6},{8,9},{10,11},{9,8... | collective-permute-start | bytes 61448 | tf_op jit(solution)/shard_map/ppermute | solution.py:514

commit v5 on v4

--- a/solution.py
+++ b/solution.py
@@ -34,8 +34,8 @@
 
 EXT = 48
 GROUP = 8 * 64
-EARLY = 10
-SECOND = 6
+EARLY = 8
+SECOND = 8
 F32 = jnp.float32
 BF16 = jnp.bfloat16
 

time: 16.1 us -> 16.2 us (level)
  transfers between devices with their start and end apart: 6 -> 6, of which waited for: 0 -> 1; matrix products, arithmetic and copies ran while one was open for 0% -> 0% of each run, Pallas kernels for 27% -> 27%
where the time goes in v5:
time: 16.2 us; the launch traced here: 16 us
  starting transfers between devices  8.3 us (51%)
  Pallas kernels  7.51 us (46%)
    ppermute x2, starting transfers between devices, shift(): lax.ppermute(block, axis, [(i, (i + distance) % count) for i in range(cou...  4.86 us
    ppermute x4, starting transfers between devices, swap(): return lax.ppermute(block, axis, ahead + [(j, i) for i, j in ahead])  3.44 us
    pallas_call x1, Pallas kernels, on_device(): call(final_kernel, vmem(10), array(NBD, 128), [pltpu.VMEM((3, 1, EXT, 128...  2.21 us
    pallas_call x1, Pallas kernels, on_device(): call(main_kernel, vmem(8) + hbm(), (array(NBD, 128), array(NBD, 128), arr...  1.6 us
    pallas_call x1, Pallas kernels, on_device(): call(early_kernel, hbm(4) + vmem(2), (array(BACK_ROWS, 128),) + packed, s...  1.29 us
    pallas_call x1, Pallas kernels, on_device(): call(fill_kernel, hbm() + vmem(3), (held(SECOND), array(EARLY * 256, 256,...  1.23 us
    pallas_call x1, Pallas kernels, on_device(): call(pack_x_kernel, hbm(4), (array(X_ROWS, 128), array(*rows.shape), arra...  1.04 us
  transfers between devices with their start and end apart: 6, of which 1 were waited for; matrix products, arithmetic and copies ran while one was open for 0% of the time, Pallas kernels for 27%

profile of v5, /device:TPU:0, one launch (start us, length us, event | category | flops | bytes accessed | tf_op | source)
XLA Modules:
  0.0 16.0 jit_solution(3136818025794690570)
XLA Ops:
  0.0 1.0 %shard_map.82 = (f32[216,128]{1,0:T(8,128)S(1)}, f32[256,128]{1,0:T(8,128)S(1)}, f32[384,128]{1,0:T(8,128)S(1)}) custom-call(s32[128]{0:T(128)} %bitcast.22, s32[2,32]{1,0:T(2,128)} %bitcast.21, f32[256,128]{1,0:T(8,128)} %bitcast.14, f32[384,128]{1,0:T(8,128)} %bitcast.13), custom_call_target="tpu_custom_call" | custom-call | flops 1000 | bytes 1000 | tf_op jit(solution)/shard_map/pallas_call | solution.py:534
  1.1 3.0 %collective-permute-start = (f32[216,128]{1,0:T(8,128)S(1)}, f32[216,128]{1,0:T(8,128)S(1)}, u32[]{:S(2)}, u32[]{:S(2)}) collective-permute-start(f32[216,128]{1,0:T(8,128)S(1)} %get-tuple-element.31), channel_id=1, source_target_pairs={{0,4},{4,8},{8,12},{12,16},{16,20},{20,24},{24,28},{28,0},{1,5},{5... | collective-permute-start | bytes 331784 | tf_op jit(solution)/shard_map/ppermute | solution.py:519
  4.0 1.3 %shard_map.83 = (f32[24,128]{1,0:T(8,128)S(1)}, f32[96,128]{1,0:T(8,128)S(1)}, f32[96,128]{1,0:T(8,128)S(1)}, s32[2,256]{1,0:T(2,128)S(1)}, s32[2,256]{1,0:T(2,128)S(1)}, /*index=5*/bf16[4096,128]{1,0:T(8,128)(2,1)S(1)}) custom-call(s32[2,64]{1,0:T(2,128)} %bitcast.19, s32[2,256]{1,0:T(2,128)} %bitcast.15, s32[2,256]{1,0:T(2,128)} %bitcast.17, ...), custom_call_target="tpu_custom_call" | custom-call | flops 1000 | bytes 1000 | tf_op jit(solution)/shard_map/pallas_call | solution.py:558
  5.3 1.9 %collective-permute-start.1 = (f32[24,128]{1,0:T(8,128)S(1)}, f32[24,128]{1,0:T(8,128)S(1)}, u32[]{:S(2)}, u32[]{:S(2)}) collective-permute-start(f32[24,128]{1,0:T(8,128)S(1)} %get-tuple-element.33), channel_id=1, source_target_pairs={{0,28},{4,0},{8,4},{12,8},{16,12},{20,16},{24,20},{28,24},{1,29},{... | collective-permute-start | bytes 36872 | tf_op jit(solution)/shard_map/ppermute | solution.py:519
  7.2 0.1 shard_map.84
  7.3 0.7 %collective-permute-start.2 = (f32[96,128]{1,0:T(8,128)S(1)}, f32[96,128]{1,0:T(8,128)S(1)}, u32[]{:S(2)}, u32[]{:S(2)}) collective-permute-start(f32[96,128]{1,0:T(8,128)S(1)} %get-tuple-element.38), channel_id=1, source_target_pairs={{1,2},{3,0},{2,1},{0,3},{5,6},{7,4},{6,5},{4,7},{9,10},{11,8},{10,... | collective-permute-start | bytes 147464 | tf_op jit(solution)/shard_map/ppermute | solution.py:514
  8.0 1.1 %collective-permute-start.3 = (f32[96,128]{1,0:T(8,128)S(1)}, f32[96,128]{1,0:T(8,128)S(1)}, u32[]{:S(2)}, u32[]{:S(2)}) collective-permute-start(f32[96,128]{1,0:T(8,128)S(1)} %get-tuple-element.39), channel_id=1, source_target_pairs={{0,1},{2,3},{1,0},{3,2},{4,5},{6,7},{5,4},{7,6},{8,9},{10,11},{9,8... | collective-permute-start | bytes 147464 | tf_op jit(solution)/shard_map/ppermute | solution.py:514
  9.1 1.2 %shard_map.86 = (bf16[4096,128]{1,0:T(8,128)(2,1)S(1)}, bf16[2048,256]{1,0:T(8,128)(2,1)S(1)}) custom-call(bf16[16384,128]{1,0:T(8,128)(2,1)} %bitcast.11, bf16[4096,128]{1,0:T(8,128)(2,1)S(1)} %get-tuple-element.45.held_early, bf16[4096,128]{1,0:T(8,128)(2,1)S(1)} %get-tuple-element.46.held_late, bf16[4096,128]{1,0:T(8,128)(2,1)S(1)} %get-tuple-element.47.second_late), custom_call_target="tpu_custom_call" | custom-call | flops 1000 | bytes 1000 | tf_op jit(solution)/shard_map/pallas_call | solution.py:573
  10.4 0.0 collective-permute-done.1.lower
  10.4 0.0 collective-permute-done.upper
  10.4 0.1 shard_map.87
  10.5 0.1 collective-permute-start.4
  10.6 1.4 %collective-permute-start.5 = (f32[40,128]{1,0:T(8,128)S(1)}, f32[40,128]{1,0:T(8,128)S(1)}, u32[]{:S(2)}, u32[]{:S(2)}) collective-permute-start(f32[40,128]{1,0:T(8,128)S(1)} %get-tuple-element.50), channel_id=1, source_target_pairs={{0,1},{2,3},{1,0},{3,2},{4,5},{6,7},{5,4},{7,6},{8,9},{10,11},{9,8... | collective-permute-start | bytes 61448 | tf_op jit(solution)/shard_map/ppermute | solution.py:514
  12.1 0.0 collective-permute-done.2.y1
  12.1 0.0 collective-permute-done.3.y0
  12.1 1.6 %shard_map.85 = (f32[256,128]{1,0:T(8,128)S(1)}, f32[256,128]{1,0:T(8,128)S(1)}, f32[3,48,128]{2,1,0:T(8,128)S(1)}, f32[256,512]{1,0:T(8,128)S(1)}, bf16[256,128...) custom-call(f32[384,128]{1,0:T(8,128)S(1)} %get-tuple-element.30.vel, f32[216,128]{1,0:T(8,128)S(1)} %collective-permute-done.upper, ...), custom_call_target="tpu_custom_call" | custom-call | flops 5000000 | bytes 5000000 | tf_op jit(solution)/shard_map/pallas_call | solution.py:584
  13.7 0.1 collective-permute-done.4.ry1
  13.8 0.0 collective-permute-done.5.ry0
  13.8 2.2 %shard_map.88 = f32[256,128]{1,0:T(8,128)} custom-call(f32[256,128]{1,0:T(8,128)S(1)} %get-tuple-element.42.lm_in, f32[256,128]{1,0:T(8,128)S(1)} %get-tuple-element.43.mm_in, f32[3,48,128]{2,1,0:T(8,128)S(1)} %get-tuple-element.44.strips, f32[40,128]{1,0:T(8,128)S(1)} %collective-permute-done.4.ry1, f32[40,128]{1,0:T(8,128)S(1)} %collective-permute-done.5.ry0, ...), custom_call_target="tpu_custom_call" | custom-call | flops 1000 | bytes 1000 | tf_op jit(solution)/shard_map/pallas_call | solution.py:605
Async XLA Ops:
  1.1 9.3 %collective-permute-start = (f32[216,128]{1,0:T(8,128)S(1)}, f32[216,128]{1,0:T(8,128)S(1)}, u32[]{:S(2)}, u32[]{:S(2)}) collective-permute-start(f32[216,128]{1,0:T(8,128)S(1)} %get-tuple-element.31), channel_id=1, source_target_pairs={{0,4},{4,8},{8,12},{12,16},{16,20},{20,24},{24,28},{28,0},{1,5},{5... | collective-permute-start | bytes 331784 | tf_op jit(solution)/shard_map/ppermute | solution.py:519
  5.3 5.0 %collective-permute-start.1 = (f32[24,128]{1,0:T(8,128)S(1)}, f32[24,128]{1,0:T(8,128)S(1)}, u32[]{:S(2)}, u32[]{:S(2)}) collective-permute-start(f32[24,128]{1,0:T(8,128)S(1)} %get-tuple-element.33), channel_id=1, source_target_pairs={{0,28},{4,0},{8,4},{12,8},{16,12},{20,16},{24,20},{28,24},{1,29},{... | collective-permute-start | bytes 36872 | tf_op jit(solution)/shard_map/ppermute | solution.py:519
  7.3 4.8 %collective-permute-start.2 = (f32[96,128]{1,0:T(8,128)S(1)}, f32[96,128]{1,0:T(8,128)S(1)}, u32[]{:S(2)}, u32[]{:S(2)}) collective-permute-start(f32[96,128]{1,0:T(8,128)S(1)} %get-tuple-element.38), channel_id=1, source_target_pairs={{1,2},{3,0},{2,1},{0,3},{5,6},{7,4},{6,5},{4,7},{9,10},{11,8},{10,... | collective-permute-start | bytes 147464 | tf_op jit(solution)/shard_map/ppermute | solution.py:514
  8.0 4.0 %collective-permute-start.3 = (f32[96,128]{1,0:T(8,128)S(1)}, f32[96,128]{1,0:T(8,128)S(1)}, u32[]{:S(2)}, u32[]{:S(2)}) collective-permute-start(f32[96,128]{1,0:T(8,128)S(1)} %get-tuple-element.39), channel_id=1, source_target_pairs={{0,1},{2,3},{1,0},{3,2},{4,5},{6,7},{5,4},{7,6},{8,9},{10,11},{9,8... | collective-permute-start | bytes 147464 | tf_op jit(solution)/shard_map/ppermute | solution.py:514
  10.5 3.3 %collective-permute-start.4 = (f32[40,128]{1,0:T(8,128)S(1)}, f32[40,128]{1,0:T(8,128)S(1)}, u32[]{:S(2)}, u32[]{:S(2)}) collective-permute-start(f32[40,128]{1,0:T(8,128)S(1)} %get-tuple-element.49), channel_id=1, source_target_pairs={{1,2},{3,0},{2,1},{0,3},{5,6},{7,4},{6,5},{4,7},{9,10},{11,8},{10,... | collective-permute-start | bytes 61448 | tf_op jit(solution)/shard_map/ppermute | solution.py:514
  10.6 3.2 %collective-permute-start.5 = (f32[40,128]{1,0:T(8,128)S(1)}, f32[40,128]{1,0:T(8,128)S(1)}, u32[]{:S(2)}, u32[]{:S(2)}) collective-permute-start(f32[40,128]{1,0:T(8,128)S(1)} %get-tuple-element.50), channel_id=1, source_target_pairs={{0,1},{2,3},{1,0},{3,2},{4,5},{6,7},{5,4},{7,6},{8,9},{10,11},{9,8... | collective-permute-start | bytes 61448 | tf_op jit(solution)/shard_map/ppermute | solution.py:514
